TPU v7x, 32 devices: a whole 2x2x4 slice. The times are simulated.
32 devices in a mesh: dp: 8 (over z, x), mp: 4 (over y, core).
Axes of the slice: x: 2, y: 2, z: 4, core: 2. Of those that a mesh axis runs over, the one named last changes fastest.
Arguments:
- tokens: bfloat16 [8, 4, 512, 768], P('dp', None, 'mp'), may hold values from -6 to 6
- memory_init: bfloat16 [20, 768], P('mp', 'dp'), may hold values from -6 to 6
- query_weight: bfloat16 [768, 768], P('dp', 'mp'), may hold values from -0.21875 to 0.21875
- query_bias: bfloat16 [768], P(('mp', 'dp')), may hold values from -3 to 3
- key_weight: bfloat16 [768, 768], P('dp', 'mp'), may hold values from -0.21875 to 0.21875
- value_weight: bfloat16 [768, 768], P('dp', 'mp'), may hold values from -0.21875 to 0.21875
- value_bias: bfloat16 [768], P(('mp', 'dp')), may hold values from -3 to 3
- out_weight: bfloat16 [768, 768], P('mp', 'dp'), may hold values from -1.75 to 1.75
- out_bias: bfloat16 [768], P(('dp', 'mp')), may hold values from -2 to 2
- first_gain: bfloat16 [768], P(('dp', 'mp')), may hold values from 0.25 to 1.75
- first_shift: bfloat16 [768], P(('dp', 'mp')), may hold values from -2 to 2
- up_weight: bfloat16 [768, 3072], P('dp', 'mp'), may hold values from -0.21875 to 0.21875
- up_bias: bfloat16 [3072], P(('mp', 'dp')), may hold values from -3 to 3
- down_weight: bfloat16 [3072, 768], P('mp', 'dp'), may hold values from -0.109375 to 0.109375
- down_bias: bfloat16 [768], P(('dp', 'mp')), may hold values from -2 to 2
- second_gain: bfloat16 [768], P(('dp', 'mp')), may hold values from 0.25 to 1.75
- second_shift: bfloat16 [768], P(('dp', 'mp')), may hold values from -2 to 2
- cotangent: bfloat16 [8, 4, 512, 768], P('dp', None, 'mp'), may hold values from -6 to 6
- group_segs: int32 [6], replicated, may hold values from 1 to 4, as said below
- chain_group: int32 [8], P('dp'), may hold values from 0 to 5
Outputs:
- layer_out: bfloat16 [8, 4, 512, 768], P('dp', None, 'mp')
- input_grad: bfloat16 [8, 4, 512, 768], P('dp', None, 'mp')
- grad_memory_init: float32 [20, 768], P('mp', 'dp')
- grad_query_weight: float32 [768, 768], P('dp', 'mp')
- grad_query_bias: float32 [768], P(('mp', 'dp'))
- grad_key_weight: float32 [768, 768], P('dp', 'mp')
- grad_value_weight: float32 [768, 768], P('dp', 'mp')
- grad_value_bias: float32 [768], P(('mp', 'dp'))
- grad_out_weight: float32 [768, 768], P('mp', 'dp')
- grad_out_bias: float32 [768], P(('dp', 'mp'))
- grad_first_gain: float32 [768], P(('dp', 'mp'))
- grad_first_shift: float32 [768], P(('dp', 'mp'))
- grad_up_weight: float32 [768, 3072], P('dp', 'mp')
- grad_up_bias: float32 [3072], P(('mp', 'dp'))
- grad_down_weight: float32 [3072, 768], P('mp', 'dp')
- grad_down_bias: float32 [768], P(('dp', 'mp'))
- grad_second_gain: float32 [768], P(('dp', 'mp'))
- grad_second_shift: float32 [768], P(('dp', 'mp'))
- memory_norms: float32 [4], replicated
Inputs may be any that keep to these rules, and one draw needn't show every extreme that they name: `group_segs`: in every draw the group of chain 0 has 4 segments; every group has 1 to 4 segments.
All inputs are finite; a program needn't handle non-finite values.
Results may differ from a plain program's by a relative error of at most 0.02.
Values may be sent and summed in bfloat16 or wider, within the bound.
No kernel may reach another device: no remote copies, remote signals or barrier semaphores. Data moves between devices by JAX's collectives and lax.ppermute only.
A program may use at most 192 MiB of HBM per device.

v0:
```python
import jax
import jax.numpy as jnp
from jax import lax
from jax.sharding import PartitionSpec as P

HD = 64


def layer_norm(resid, gain, shift):
    center = resid - jnp.mean(resid, axis=-1, keepdims=True)
    spread = jnp.mean(center * center, axis=-1, keepdims=True)
    return center * lax.rsqrt(spread + 1e-05) * gain + shift


def exact_gelu(pre):
    return jax.nn.gelu(pre, approximate=False)


def contract_rows(left, right):
    return lax.dot_general(
        left, right, (((0,), (0,)), ((), ())), preferred_element_type=jnp.float32
    )


def times_transpose(left, weight):
    return lax.dot_general(
        left, weight, (((1,), (1,)), ((), ())), preferred_element_type=jnp.float32
    )


def add_all(total, part):
    if total is None:
        return part
    return tuple((first + second for first, second in zip(total, part)))


def forward_segment(memory_own, tokens_own, weights, shared):
    (
        query_full,
        key_full,
        value_full,
        up_full,
        query_add,
        value_add,
        up_add,
        out_full,
        down_full,
        spare,
    ) = weights
    out_add, first_gain, first_shift, down_add, second_gain, second_shift = shared
    mem_local = memory_own.shape[0]
    mem_rows, tok_rows = (
        lax.all_gather(memory_own.astype(jnp.bfloat16), "mp", axis=0, tiled=True),
        lax.all_gather(tokens_own, "mp", axis=0, tiled=True),
    )
    mem_all = mem_rows.shape[0]
    rounded = jnp.concatenate([mem_rows, tok_rows], axis=0)
    count = rounded.shape[0]
    scale = HD ** (-0.5)
    query = (
        (
            jnp.dot(rounded, query_full, preferred_element_type=jnp.float32)
            + query_add.astype(jnp.float32)
        )
        .astype(jnp.bfloat16)
        .reshape(count, -1, HD)
    )
    keys = (
        jnp.dot(rounded, key_full, preferred_element_type=jnp.float32)
        .astype(jnp.bfloat16)
        .reshape(count, -1, HD)
    )
    values = (
        (
            jnp.dot(rounded, value_full, preferred_element_type=jnp.float32)
            + value_add.astype(jnp.float32)
        )
        .astype(jnp.bfloat16)
        .reshape(count, -1, HD)
    )
    scores = jnp.einsum("qhd,khd->hqk", query, keys, preferred_element_type=jnp.float32) * scale
    peak = jnp.max(scores, axis=-1, keepdims=True)
    expo = jnp.exp(scores - peak)
    total = jnp.sum(expo, axis=-1, keepdims=True)
    logsum = peak + jnp.log(total)
    probs = (expo / total).astype(jnp.bfloat16)
    attended = (
        jnp.einsum("hqk,khd->qhd", probs, values, preferred_element_type=jnp.float32)
        .reshape(count, -1)
        .astype(jnp.bfloat16)
    )
    branch = jnp.dot(attended, out_full, preferred_element_type=jnp.float32)
    part_mem, part_tok = (
        lax.psum_scatter(
            branch[:mem_all].astype(jnp.bfloat16), "mp", scatter_dimension=0, tiled=True
        ).astype(jnp.float32),
        lax.psum_scatter(
            branch[mem_all:].astype(jnp.bfloat16), "mp", scatter_dimension=0, tiled=True
        ).astype(jnp.float32),
    )
    own_rows = jnp.concatenate([memory_own, tokens_own.astype(jnp.float32)], axis=0)
    resid_one = own_rows + jnp.concatenate([part_mem, part_tok], axis=0) + out_add
    normed_one = layer_norm(resid_one, first_gain, first_shift)
    norm_mem, norm_tok = (
        lax.all_gather(normed_one[:mem_local].astype(jnp.bfloat16), "mp", axis=0, tiled=True),
        lax.all_gather(normed_one[mem_local:].astype(jnp.bfloat16), "mp", axis=0, tiled=True),
    )
    normed_all = jnp.concatenate([norm_mem, norm_tok], axis=0)
    pre = jnp.dot(normed_all, up_full, preferred_element_type=jnp.float32) + up_add.astype(
        jnp.float32
    )
    inner = exact_gelu(pre).astype(jnp.bfloat16)
    branch_two = jnp.dot(inner, down_full, preferred_element_type=jnp.float32)
    ffn_mem, ffn_tok = (
        lax.psum_scatter(
            branch_two[:mem_all].astype(jnp.bfloat16), "mp", scatter_dimension=0, tiled=True
        ).astype(jnp.float32),
        lax.psum_scatter(
            branch_two[mem_all:].astype(jnp.bfloat16), "mp", scatter_dimension=0, tiled=True
        ).astype(jnp.float32),
    )
    resid_two = normed_one + jnp.concatenate([ffn_mem, ffn_tok], axis=0) + down_add
    normed_two = layer_norm(resid_two, second_gain, second_shift)
    kept = (
        rounded,
        query,
        keys,
        values,
        logsum,
        attended,
        resid_one,
        normed_all,
        pre,
        inner,
        resid_two,
    )
    return (normed_two[:mem_local], normed_two[mem_local:], kept)


def backward_segment(grad_memory, grad_tokens, kept, weights, shared):
    (
        query_full,
        key_full,
        value_full,
        up_full,
        query_add,
        value_add,
        up_add,
        out_full,
        down_full,
        spare,
    ) = weights
    out_add, first_gain, first_shift, down_add, second_gain, second_shift = shared
    rounded, query, keys, values, logsum, attended, resid_one, normed_all, pre, inner, resid_two = (
        kept
    )
    mem_local = grad_memory.shape[0]
    mem_all = mem_local * lax.axis_size("mp")
    count = rounded.shape[0]
    scale = HD ** (-0.5)
    pull_two = jax.vjp(layer_norm, resid_two, second_gain, second_shift)[1]
    grad_resid_two, grad_second_gain, grad_second_shift = pull_two(
        jnp.concatenate([grad_memory, grad_tokens], axis=0)
    )
    grad_mem_rows, grad_tok_rows = (
        lax.all_gather(grad_resid_two[:mem_local].astype(jnp.bfloat16), "mp", axis=0, tiled=True),
        lax.all_gather(grad_resid_two[mem_local:].astype(jnp.bfloat16), "mp", axis=0, tiled=True),
    )
    grad_branch_two = jnp.concatenate([grad_mem_rows, grad_tok_rows], axis=0)
    grad_down = contract_rows(inner, grad_branch_two)
    grad_inner = times_transpose(grad_branch_two, down_full)
    grad_pre = jax.vjp(exact_gelu, pre)[1](grad_inner)[0].astype(jnp.bfloat16)
    grad_up = contract_rows(normed_all, grad_pre)
    grad_up_add = jnp.sum(grad_pre.astype(jnp.float32), axis=0)
    back_ffn = times_transpose(grad_pre, up_full)
    back_mem, back_tok = (
        lax.psum_scatter(
            back_ffn[:mem_all].astype(jnp.bfloat16), "mp", scatter_dimension=0, tiled=True
        ).astype(jnp.float32),
        lax.psum_scatter(
            back_ffn[mem_all:].astype(jnp.bfloat16), "mp", scatter_dimension=0, tiled=True
        ).astype(jnp.float32),
    )
    grad_normed_one = grad_resid_two + jnp.concatenate([back_mem, back_tok], axis=0)
    pull_one = jax.vjp(layer_norm, resid_one, first_gain, first_shift)[1]
    grad_resid_one, grad_first_gain, grad_first_shift = pull_one(grad_normed_one)
    attn_mem, attn_tok = (
        lax.all_gather(grad_resid_one[:mem_local].astype(jnp.bfloat16), "mp", axis=0, tiled=True),
        lax.all_gather(grad_resid_one[mem_local:].astype(jnp.bfloat16), "mp", axis=0, tiled=True),
    )
    grad_branch = jnp.concatenate([attn_mem, attn_tok], axis=0)
    grad_out = contract_rows(attended, grad_branch)
    grad_attended = (
        times_transpose(grad_branch, out_full).astype(jnp.bfloat16).reshape(count, -1, HD)
    )
    scores = jnp.einsum("qhd,khd->hqk", query, keys, preferred_element_type=jnp.float32) * scale
    probs = jnp.exp(scores - logsum)
    grad_values = (
        jnp.einsum(
            "hqk,qhd->khd",
            probs.astype(jnp.bfloat16),
            grad_attended,
            preferred_element_type=jnp.float32,
        )
        .astype(jnp.bfloat16)
        .reshape(count, -1)
    )
    grad_probs = jnp.einsum(
        "qhd,khd->hqk", grad_attended, values, preferred_element_type=jnp.float32
    )
    grad_scores = (
        probs * (grad_probs - jnp.sum(grad_probs * probs, axis=-1, keepdims=True))
    ).astype(jnp.bfloat16)
    grad_query = (
        (jnp.einsum("hqk,khd->qhd", grad_scores, keys, preferred_element_type=jnp.float32) * scale)
        .astype(jnp.bfloat16)
        .reshape(count, -1)
    )
    grad_keys = (
        (jnp.einsum("hqk,qhd->khd", grad_scores, query, preferred_element_type=jnp.float32) * scale)
        .astype(jnp.bfloat16)
        .reshape(count, -1)
    )
    grad_query_w = contract_rows(rounded, grad_query)
    grad_key_w = contract_rows(rounded, grad_keys)
    grad_value_w = contract_rows(rounded, grad_values)
    grad_query_add = jnp.sum(grad_query.astype(jnp.float32), axis=0)
    grad_value_add = jnp.sum(grad_values.astype(jnp.float32), axis=0)
    back_rows = (
        times_transpose(grad_query, query_full)
        + times_transpose(grad_keys, key_full)
        + times_transpose(grad_values, value_full)
    )
    in_mem, in_tok = (
        lax.psum_scatter(
            back_rows[:mem_all].astype(jnp.bfloat16), "mp", scatter_dimension=0, tiled=True
        ).astype(jnp.float32),
        lax.psum_scatter(
            back_rows[mem_all:].astype(jnp.bfloat16), "mp", scatter_dimension=0, tiled=True
        ).astype(jnp.float32),
    )
    grad_hidden = grad_resid_one + jnp.concatenate([in_mem, in_tok], axis=0)
    big_part = (
        grad_query_w,
        grad_key_w,
        grad_value_w,
        grad_up,
        grad_query_add,
        grad_value_add,
        grad_up_add,
        grad_out,
        grad_down,
    )
    small_part = (
        jnp.sum(grad_resid_one, axis=0),
        grad_first_gain,
        grad_first_shift,
        jnp.sum(grad_resid_two, axis=0),
        grad_second_gain,
        grad_second_shift,
    )
    return (grad_hidden[:mem_local], grad_hidden[mem_local:], big_part, small_part)


def body(
    tokens,
    memory_init,
    query_weight,
    query_bias,
    key_weight,
    value_weight,
    value_bias,
    out_weight,
    out_bias,
    first_gain,
    first_shift,
    up_weight,
    up_bias,
    down_weight,
    down_bias,
    second_gain,
    second_shift,
    cotangent,
    group_segs,
    chain_group,
):

    def gather_weights():
        return (
            lax.all_gather(query_weight, "dp", axis=0, tiled=True),
            lax.all_gather(key_weight, "dp", axis=0, tiled=True),
            lax.all_gather(value_weight, "dp", axis=0, tiled=True),
            lax.all_gather(up_weight, "dp", axis=0, tiled=True),
            lax.all_gather(query_bias, "dp", axis=0, tiled=True),
            lax.all_gather(value_bias, "dp", axis=0, tiled=True),
            lax.all_gather(up_bias, "dp", axis=0, tiled=True),
            lax.all_gather(out_weight, "dp", axis=1, tiled=True),
            lax.all_gather(down_weight, "dp", axis=1, tiled=True),
            lax.all_gather(memory_init, "dp", axis=1, tiled=True),
        )

    chains_here = tokens.shape[0]
    segments = tokens.shape[1]
    chains_all = chains_here * lax.axis_size("dp")
    gathered = (
        lax.all_gather(out_bias, ("dp", "mp"), axis=0, tiled=True),
        lax.all_gather(first_gain, ("dp", "mp"), axis=0, tiled=True),
        lax.all_gather(first_shift, ("dp", "mp"), axis=0, tiled=True),
        lax.all_gather(down_bias, ("dp", "mp"), axis=0, tiled=True),
        lax.all_gather(second_gain, ("dp", "mp"), axis=0, tiled=True),
        lax.all_gather(second_shift, ("dp", "mp"), axis=0, tiled=True),
    )
    shared = tuple((item.astype(jnp.float32) for item in gathered))
    match = chain_group[:, None] == jnp.arange(group_segs.shape[0], dtype=jnp.int32)[None, :]
    seg_count = jnp.sum(jnp.where(match, group_segs[None, :], 0), axis=1)
    big_total = None
    small_total = None
    flags = [(index < seg_count[0]).astype(jnp.float32) for index in range(segments)]
    memory = None
    kept_list = []
    outputs = []
    terms = []
    for index in range(segments):
        weights = gather_weights()
        if index == 0:
            memory = weights[9].astype(jnp.float32)
        memory, token_out, kept = forward_segment(memory, tokens[0, index], weights, shared)
        kept_list.append(kept)
        outputs.append(token_out * flags[index])
        mem_total = memory.shape[0] * lax.axis_size("mp")
        terms.append(
            flags[index] * jnp.sum(memory * memory) / (mem_total * memory.shape[1] * chains_all)
        )
    chain_outputs = [jnp.stack(outputs)]
    chain_terms = [jnp.stack(terms)]
    grad_memory = jnp.zeros_like(memory)
    token_grads = [None] * segments
    for index in reversed(range(segments)):
        weights = gather_weights()
        grad_tokens = cotangent[0, index].astype(jnp.float32) * flags[index]
        grad_memory, grad_tok, big_part, small_part = backward_segment(
            grad_memory, grad_tokens, kept_list[index], weights, shared
        )
        token_grads[index] = grad_tok
        small_total = add_all(small_total, small_part)
        memory_part = grad_memory if index == 0 else jnp.zeros_like(grad_memory)
        parts = big_part + (memory_part,)
        big_total = add_all(
            big_total,
            (
                lax.psum_scatter(parts[0], "dp", scatter_dimension=0, tiled=True),
                lax.psum_scatter(parts[1], "dp", scatter_dimension=0, tiled=True),
                lax.psum_scatter(parts[2], "dp", scatter_dimension=0, tiled=True),
                lax.psum_scatter(parts[3], "dp", scatter_dimension=0, tiled=True),
                lax.psum_scatter(parts[4], "dp", scatter_dimension=0, tiled=True),
                lax.psum_scatter(parts[5], "dp", scatter_dimension=0, tiled=True),
                lax.psum_scatter(parts[6], "dp", scatter_dimension=0, tiled=True),
                lax.psum_scatter(parts[7], "dp", scatter_dimension=1, tiled=True),
                lax.psum_scatter(parts[8], "dp", scatter_dimension=1, tiled=True),
                lax.psum_scatter(parts[9], "dp", scatter_dimension=1, tiled=True),
            ),
        )
    chain_grads = [jnp.stack(token_grads)]
    small_done = lax.psum_scatter(small_total, ("dp", "mp"), scatter_dimension=0, tiled=True)
    norms = lax.psum(jnp.sum(jnp.stack(chain_terms), axis=0), ("dp", "mp"))
    layer_out = jnp.stack(chain_outputs).astype(jnp.bfloat16)
    input_grad = jnp.stack(chain_grads).astype(jnp.bfloat16)
    return (
        layer_out,
        input_grad,
        big_total[9],
        big_total[0],
        big_total[4],
        big_total[1],
        big_total[2],
        big_total[5],
        big_total[7],
        small_done[0],
        small_done[1],
        small_done[2],
        big_total[3],
        big_total[6],
        big_total[8],
        small_done[3],
        small_done[4],
        small_done[5],
        norms,
    )


def solution(mesh):
    in_specs = (
        P("dp", None, "mp", None),
        P("mp", "dp"),
        P("dp", "mp"),
        P(("mp", "dp")),
        P("dp", "mp"),
        P("dp", "mp"),
        P(("mp", "dp")),
        P("mp", "dp"),
        P(("dp", "mp")),
        P(("dp", "mp")),
        P(("dp", "mp")),
        P("dp", "mp"),
        P(("mp", "dp")),
        P("mp", "dp"),
        P(("dp", "mp")),
        P(("dp", "mp")),
        P(("dp", "mp")),
        P("dp", None, "mp", None),
        P(),
        P("dp"),
    )
    out_specs = (
        P("dp", None, "mp", None),
        P("dp", None, "mp", None),
        P("mp", "dp"),
        P("dp", "mp"),
        P(("mp", "dp")),
        P("dp", "mp"),
        P("dp", "mp"),
        P(("mp", "dp")),
        P("mp", "dp"),
        P(("dp", "mp")),
        P(("dp", "mp")),
        P(("dp", "mp")),
        P("dp", "mp"),
        P(("mp", "dp")),
        P("mp", "dp"),
        P(("dp", "mp")),
        P(("dp", "mp")),
        P(("dp", "mp")),
        P(),
    )
    return jax.shard_map(body, mesh=mesh, in_specs=in_specs, out_specs=out_specs, check_vma=False)
```

profile of v0, /device:TPU:0, one launch (start us, length us, event | category | flops | bytes accessed | tf_op | source)
XLA Modules:
  0.0 1503.8 jit_solution(4248616646348663074)
XLA Ops:
  10.7 33.0 %all_gather.198 = bf16[768,192]{1,0:T(8,128)(2,1)S(1)} all-gather(bf16[96,192]{1,0:T(8,128)(2,1)} %param.25), channel_id=1, replica_groups=mesh['dp'=8,'mp'=4] {'dp'}, dimensions={0}, use_global_device_ids=true | all-gather | bytes 331776 | tf_op jit(solution)/shard_map/all_gather | solution.py:292
  46.2 21.4 %all-reduce.54 = (bf16[768]{0:T(1024)(128)(2,1)S(1)}, bf16[192]{0:T(256)(128)(2,1)S(1)}, bf16[192]{0:T(256)(128)(2,1)S(1)}) all-reduce(bf16[768]{0:T(1024)(128)(2,1)S(1)} %dynamic-update-slice.5, bf16[192]{0:T(256)(128)(2,1)S(1)} %dynamic-update-slice, bf16[192]{0:T(256)(128)(2,1)S(1)} %dynamic-update-slice.1), channel_id=1, replica_groups=mesh['dp'=8,'mp'=4] {'dp'}, use_global_device_ids=true, to_apply=%add.6 | all-reduce | flops 1152 | bytes 4608
  78.9 26.0 %all-gather.4 = bf16[8,96,5]{1,2,0:T(8,128)(2,1)S(1)} all-gather(bf16[1,96,5]{1,2,0:T(8,128)(2,1)S(1)} %bitcast.430), channel_id=1, replica_groups=mesh['dp'=8,'mp'=4] {'dp'}, dimensions={0}, use_global_device_ids=true | all-gather | bytes 8640 | tf_op jit(solution)/shard_map/all_gather | solution.py:299
  110.2 31.0 %all_gather.200 = bf16[768,192]{1,0:T(8,128)(2,1)S(1)} all-gather(bf16[96,192]{1,0:T(8,128)(2,1)S(1)} %copy-done.172), channel_id=1, replica_groups=mesh['dp'=8,'mp'=4] {'dp'}, dimensions={0}, use_global_device_ids=true | all-gather | bytes 331776 | tf_op jit(solution)/shard_map/all_gather | solution.py:290
  141.3 31.0 %all_gather.202 = bf16[768,192]{1,0:T(8,128)(2,1)S(1)} all-gather(bf16[96,192]{1,0:T(8,128)(2,1)S(1)} %copy-done.173), channel_id=1, replica_groups=mesh['dp'=8,'mp'=4] {'dp'}, dimensions={0}, use_global_device_ids=true | all-gather | bytes 331776 | tf_op jit(solution)/shard_map/all_gather | solution.py:291
  172.4 31.0 %all_gather.203 = bf16[192,768]{0,1:T(8,128)(2,1)S(1)} all-gather(bf16[192,96]{0,1:T(8,128)(2,1)S(1)} %copy.75), channel_id=1, replica_groups=mesh['dp'=8,'mp'=4] {'dp'}, dimensions={1}, use_global_device_ids=true | all-gather | bytes 331776 | tf_op jit(solution)/shard_map/all_gather | solution.py:297
  224.7 37.6 %all-reduce.53 = (bf16[768]{0:T(1024)(128)(2,1)S(1)}, bf16[768]{0:T(1024)(128)(2,1)S(1)}, bf16[768]{0:T(1024)(128)(2,1)S(1)}, bf16[768]{0:T(1024)(128)(2,1)S(1)}...) all-reduce(bf16[768]{0:T(1024)(128)(2,1)S(1)} %dynamic-update-slice, ...), channel_id=1, replica_groups=mesh['dp'=8,'mp'=4] {'dp','mp'}, use_global_device_ids=true, to_apply=%add.5 | all-reduce | flops 4608 | bytes 18432
  273.1 9.6 all_gather.208
  308.7 11.7 all-gather.1
  397.1 11.1 all-gather.2
  443.9 8.8 reduce-scatter.68.cloned.1.call-done
  492.0 11.5 all-gather.3
  806.1 8.9 reduce-scatter.82.cloned.1.call-done
  911.6 8.9 reduce-scatter.86.cloned.1.call-done
  960.7 8.9 reduce-scatter.88.cloned.1.call-done
  974.6 8.8 all_gather.242
  1067.0 21.7 %all-reduce.52 = (f32[192]{0:T(256)S(1)}, f32[192]{0:T(256)S(1)}, f32[768]{0:T(1024)S(1)}) all-reduce(f32[192]{0:T(256)S(1)} %reshape.623, f32[192]{0:T(256)S(1)} %reshape.624, f32[768]{0:T(1024)S(1)} %add_add_fusion.15), channel_id=67, replica_groups=mesh['dp'=8,'mp'=4] {'dp'}, use_global_device_ids=true, to_apply=%region_83.84.clone | all-reduce | flops 1152 | bytes 9216
  1090.1 37.9 %all-reduce.51 = (f32[768]{0:T(1024)S(1)}, f32[768]{0:T(1024)S(1)}, f32[768]{0:T(1024)S(1)}, f32[768]{0:T(1024)S(1)}, f32[768]{0:T(1024)S(1)}, /*index=5*/f32[768]{0:T(1024)S(1)}, f32[4]{0:T(128)}) all-reduce(f32[768]{0:T(1024)S(1)} %add_add_fusion.21, ...), channel_id=72, replica_groups=mesh['dp'=8,'mp'=4] {'dp','mp'}, use_global_device_ids=true, to_apply=%region_114.115.clone | all-reduce | flops 4612 | bytes 36896
  1135.7 19.6 %reduce-scatter.102.cloned.1.call-done = f32[96,5]{1,0:T(8,128)} async-done(((f32[768,5]{1,0:T(8,128)}), f32[96,5]{1,0:T(8,128)}) %reduce-scatter.102.cloned.1.call-update) | async-done | bytes 1936
  1156.8 64.3 %reduce-scatter.92.cloned.1.call-done = f32[96,192]{1,0:T(8,128)} async-done(((f32[768,192]{1,0:T(8,128)}), f32[96,192]{1,0:T(8,128)}) %reduce-scatter.92.cloned.1.call-update) | async-done | bytes 73744 | tf_op jit(solution)/shard_map/reduce_scatter | solution.py:351
  1221.1 65.2 %reduce-scatter.94.cloned.1.call-done = f32[96,192]{1,0:T(8,128)} async-done(((f32[768,192]{1,0:T(8,128)}), f32[96,192]{1,0:T(8,128)}) %reduce-scatter.94.cloned.1.call-update) | async-done | bytes 73744 | tf_op jit(solution)/shard_map/reduce_scatter | solution.py:352
  1286.3 65.7 %reduce-scatter.96.cloned.1.call-done = f32[96,192]{1,0:T(8,128)} async-done(((f32[768,192]{1,0:T(8,128)}), f32[96,192]{1,0:T(8,128)}) %reduce-scatter.96.cloned.1.call-update) | async-done | bytes 73744 | tf_op jit(solution)/shard_map/reduce_scatter | solution.py:353
  1352.0 72.1 %reduce-scatter.98.cloned.1.call-done = f32[96,768]{1,0:T(8,128)} async-done(((f32[768,768]{1,0:T(8,128)}), f32[96,768]{1,0:T(8,128)}) %reduce-scatter.98.cloned.1.call-update) | async-done | bytes 294928 | tf_op jit(solution)/shard_map/reduce_scatter | solution.py:354
  1424.1 72.1 %reduce-scatter.100.cloned.1.call-done = f32[768,96]{0,1:T(8,128)} async-done(((f32[768,768]{0,1:T(8,128)}), f32[768,96]{0,1:T(8,128)}) %reduce-scatter.100.cloned.1.call-update) | async-done | bytes 294928 | tf_op jit(solution)/shard_map/reduce_scatter | solution.py:359
  (1193 shorter events, 756.2 us)
Async XLA Ops:
  8.0 255.9 %reduce-scatter.60.cloned.1.call-start = ((), (), s32[]{:S(2)}) async-start(), calls=%async_computation.23 | async-start | bytes 983040 | tf_op jit(solution)/shard_map/reduce_scatter | solution.py:97
  210.5 72.1 %all-gather.24.cloned.1.call-start = ((), (), s32[]{:S(2)}) async-start(), calls=%async_computation.24 | async-start | bytes 1327104 | tf_op jit(solution)/shard_map/all_gather | solution.py:293
  211.1 82.1 %all-gather.26.cloned.1.call-start = ((), (), s32[]{:S(2)}) async-start(), calls=%async_computation.25 | async-start | bytes 1327104 | tf_op jit(solution)/shard_map/all_gather | solution.py:298
  223.2 97.7 %reduce-scatter.62.cloned.1.call-start = ((), (), s32[]{:S(2)}) async-start(), calls=%async_computation.26 | async-start | bytes 983040 | tf_op jit(solution)/shard_map/reduce_scatter | solution.py:118
  336.9 72.3 %reduce-scatter.66.cloned.1.call-start = ((), (), s32[]{:S(2)}) async-start(), calls=%async_computation.28 | async-start | bytes 983040 | tf_op jit(solution)/shard_map/reduce_scatter | solution.py:118
  383.7 69.0 %reduce-scatter.68.cloned.1.call-start = ((), (), s32[]{:S(2)}) async-start(), calls=%async_computation.29 | async-start | bytes 983040 | tf_op jit(solution)/shard_map/reduce_scatter | solution.py:97
  428.6 75.6 %reduce-scatter.70.cloned.1.call-start = ((), (), s32[]{:S(2)}) async-start(), calls=%async_computation.30 | async-start | bytes 983040 | tf_op jit(solution)/shard_map/reduce_scatter | solution.py:118
  478.6 68.0 %reduce-scatter.72.cloned.1.call-start = ((), (), s32[]{:S(2)}) async-start(), calls=%async_computation.31 | async-start | bytes 983040 | tf_op jit(solution)/shard_map/reduce_scatter | solution.py:97
  522.5 77.0 %reduce-scatter.74.cloned.1.call-start = ((), (), s32[]{:S(2)}) async-start(), calls=%async_computation.32 | async-start | bytes 983040 | tf_op jit(solution)/shard_map/reduce_scatter | solution.py:118
  573.7 75.6 %reduce-scatter.76.cloned.1.call-start = ((), (), s32[]{:S(2)}) async-start(), calls=%async_computation.33 | async-start | bytes 983040 | tf_op jit(solution)/shard_map/reduce_scatter | solution.py:180
  625.3 81.9 %reduce-scatter.78.cloned.1.call-start = ((), (), s32[]{:S(2)}) async-start(), calls=%async_computation.34 | async-start | bytes 983040 | tf_op jit(solution)/shard_map/reduce_scatter | solution.py:238
  683.4 75.1 %reduce-scatter.80.cloned.1.call-start = ((), (), s32[]{:S(2)}) async-start(), calls=%async_computation.35 | async-start | bytes 983040 | tf_op jit(solution)/shard_map/reduce_scatter | solution.py:180
  734.7 80.3 %reduce-scatter.82.cloned.1.call-start = ((), (), s32[]{:S(2)}) async-start(), calls=%async_computation.36 | async-start | bytes 983040 | tf_op jit(solution)/shard_map/reduce_scatter | solution.py:238
  791.2 73.8 %reduce-scatter.84.cloned.1.call-start = ((), (), s32[]{:S(2)}) async-start(), calls=%async_computation.37 | async-start | bytes 983040 | tf_op jit(solution)/shard_map/reduce_scatter | solution.py:180
  841.2 79.2 %reduce-scatter.86.cloned.1.call-start = ((), (), s32[]{:S(2)}) async-start(), calls=%async_computation.38 | async-start | bytes 983040 | tf_op jit(solution)/shard_map/reduce_scatter | solution.py:238
  896.7 72.9 %reduce-scatter.88.cloned.1.call-start = ((), (), s32[]{:S(2)}) async-start(), calls=%async_computation.39 | async-start | bytes 983040 | tf_op jit(solution)/shard_map/reduce_scatter | solution.py:180
  945.8 79.7 %reduce-scatter.90.cloned.1.call-start = ((), (), s32[]{:S(2)}) async-start(), calls=%async_computation.40 | async-start | bytes 983040 | tf_op jit(solution)/shard_map/reduce_scatter | solution.py:238
  1001.7 130.4 %reduce-scatter.104.cloned.1.call-start = ((), (), s32[]{:S(2)}) async-start(), calls=%async_computation.47 | async-start | bytes 884736
  1006.8 148.5 %reduce-scatter.102.cloned.1.call-start = ((), (), s32[]{:S(2)}) async-start(), calls=%async_computation.46 | async-start | bytes 442368
  1028.4 192.7 %reduce-scatter.92.cloned.1.call-start = ((), (), s32[]{:S(2)}) async-start(), calls=%async_computation.41 | async-start | bytes 884736 | tf_op jit(solution)/shard_map/reduce_scatter | solution.py:351
  1031.3 255.0 %reduce-scatter.94.cloned.1.call-start = ((), (), s32[]{:S(2)}) async-start(), calls=%async_computation.42 | async-start | bytes 884736 | tf_op jit(solution)/shard_map/reduce_scatter | solution.py:352
  1036.5 315.5 %reduce-scatter.96.cloned.1.call-start = ((), (), s32[]{:S(2)}) async-start(), calls=%async_computation.43 | async-start | bytes 884736 | tf_op jit(solution)/shard_map/reduce_scatter | solution.py:353
  1042.0 382.1 %reduce-scatter.98.cloned.1.call-start = ((), (), s32[]{:S(2)}) async-start(), calls=%async_computation.44 | async-start | bytes 2654208 | tf_op jit(solution)/shard_map/reduce_scatter | solution.py:354
  1049.0 447.2 %reduce-scatter.100.cloned.1.call-start = ((), (), s32[]{:S(2)}) async-start(), calls=%async_computation.45 | async-start | bytes 2654208 | tf_op jit(solution)/shard_map/reduce_scatter | solution.py:359
  (349 other events, 4373.3 us)
Sparse Core Ops, SparseCore 0:
  210.7 19.9 reduce-scatter.59
  296.8 24.0 reduce-scatter.61
  337.0 21.5 reduce-scatter.63
  383.8 25.3 reduce-scatter.65
  428.7 23.9 reduce-scatter.67
  478.8 25.3 reduce-scatter.69
  522.6 23.9 reduce-scatter.71
  573.9 23.6 reduce-scatter.73
  625.4 23.9 reduce-scatter.75
  683.5 23.6 reduce-scatter.77
  734.8 23.6 reduce-scatter.79
  791.3 23.6 reduce-scatter.81
  841.4 23.6 reduce-scatter.83
  896.8 23.6 reduce-scatter.85
  946.0 23.6 reduce-scatter.87
  1001.8 23.6 reduce-scatter.89
  1028.6 62.7 reduce-scatter.103
  1094.8 60.4 reduce-scatter.101
  1159.5 61.5 reduce-scatter.91
  1224.8 61.4 reduce-scatter.93
  1290.5 61.4 reduce-scatter.95
  1356.1 67.9 reduce-scatter.97
  1428.2 68.0 reduce-scatter.99
Sparse Core Ops, SparseCore 1:
  213.4 37.5 all-gather.23
  253.3 39.9 all-gather.25
where the time goes:
time: 1520 us; the launch traced here: 1500 us
  blocking collectives  626 us (41%)
  waiting for transfers between devices  445 us (29%)
  matrix products  146 us (10%)
  local copies, waits for them, and re-layouts  106 us (7%)
  starting transfers between devices  80.6 us (5%)
  other arithmetic  70.5 us (5%)
  between operations  29.8 us (2%)
    unnamed x20, blocking collectives  243 us
    unnamed x34, starting transfers between devices  79.2 us
    unnamed x744, local copies, waits for them, and re-layouts  75.2 us
    reduce_scatter x1, waiting for transfers between devices, body(): lax.psum_scatter(parts[8], 'dp', scatter_dimension=1, tiled=True)  72.1 us
    reduce_scatter x1, waiting for transfers between devices, body(): lax.psum_scatter(parts[3], 'dp', scatter_dimension=0, tiled=True)  72.1 us
    reduce_scatter x1, waiting for transfers between devices, body(): lax.psum_scatter(parts[2], 'dp', scatter_dimension=0, tiled=True)  65.7 us
    reduce_scatter x1, waiting for transfers between devices, body(): lax.psum_scatter(parts[1], 'dp', scatter_dimension=0, tiled=True)  65.2 us
    reduce_scatter x1, waiting for transfers between devices, body(): lax.psum_scatter(parts[0], 'dp', scatter_dimension=0, tiled=True)  64.3 us
  transfers between devices with their start and end apart: 57, of which 26 were waited for; matrix products, arithmetic and copies ran while one was open for 15% of the time, Pallas kernels for 0%

commit v1 on v0

v1 whole, which is shorter than its diff:
```python
import functools

import jax
import jax.numpy as jnp
from jax import lax
from jax.experimental import pallas as pl
from jax.experimental.pallas import tpu as pltpu
from jax.sharding import PartitionSpec as P

HD = 64
HPB = 3
BF = jnp.bfloat16
F32 = jnp.float32
VMEM_LIMIT = 60 * 1024 * 1024
NEG = -1e30


def nn(a, b):
    return lax.dot_general(a, b, (((1,), (0,)), ((), ())), preferred_element_type=F32)


def nt(a, b):
    return lax.dot_general(a, b, (((1,), (1,)), ((), ())), preferred_element_type=F32)


def norm_stats(r):
    mean = jnp.mean(r, axis=-1, keepdims=True)
    c = r - mean
    inv = lax.rsqrt(jnp.mean(c * c, axis=-1, keepdims=True) + 1e-05)
    return c * inv, inv


def norm_back(g, xh, inv):
    return inv * (
        g - jnp.mean(g, axis=-1, keepdims=True) - xh * jnp.mean(g * xh, axis=-1, keepdims=True)
    )


def gelu_both(f):
    cdf = 0.5 + 0.5 * lax.erf(f * (0.5**0.5))
    pdf = jnp.exp(-0.5 * f * f) * ((2.0 * jnp.pi) ** -0.5)
    return f * cdf, cdf + f * pdf


def rows_mask(shape, count):
    return lax.broadcasted_iota(jnp.int32, shape, 0) < count


def any_spec():
    return pl.BlockSpec(memory_space=pl.ANY)


def vm_spec():
    return pl.BlockSpec(memory_space=pltpu.VMEM)


def params():
    return pltpu.CompilerParams(vmem_limit_bytes=VMEM_LIMIT)


def qkv_kernel(tok_ref, w_ref, qkvb_ref, out_ref, wc, sem):
    nb = w_ref.shape[0]
    d = tok_ref.shape[1]
    copies = [
        pltpu.make_async_copy(w_ref.at[j, :, 0:d], wc.at[j], sem.at[j]) for j in range(nb)
    ]
    for c in copies:
        c.start()
    w3 = 3 * HPB * HD
    for j in range(nb):
        copies[j].wait()
        acc = nn(tok_ref[...], wc[j, :, 0:w3]) + qkvb_ref[j]
        out_ref[j, :, 0 : HPB * HD] = (acc[:, 0 : HPB * HD].astype(BF) * 0.125).astype(BF)
        out_ref[j, :, HPB * HD : w3] = acc[:, HPB * HD : w3].astype(BF)


def qkv_call(tok, w, qkvb):
    nb, d, _ = w.shape
    s = tok.shape[0]
    return pl.pallas_call(
        qkv_kernel,
        out_shape=jax.ShapeDtypeStruct((nb, s, 3 * HPB * HD), BF),
        in_specs=[vm_spec(), any_spec(), vm_spec()],
        out_specs=vm_spec(),
        scratch_shapes=[pltpu.VMEM((nb, d, d), BF), pltpu.SemaphoreType.DMA((nb,))],
        compiler_params=params(),
        cost_estimate=pl.CostEstimate(
            flops=2 * s * d * 3 * d, bytes_accessed=8 * d * d, transcendentals=0
        ),
        name="qkv",
    )(tok, w, qkvb)


def load_w(w_ref, wv, sem):
    nb = w_ref.shape[0]
    d = w_ref.shape[1]
    copies = {}
    for part in range(3):
        for j in range(nb):
            cols = slice(part * d, (part + 1) * d)
            copies[part, j] = pltpu.make_async_copy(
                w_ref.at[j, :, cols], wv.at[j, :, cols], sem.at[part, j]
            )
            copies[part, j].start()
    return copies


def mem_forward_kernel(
    nmem, save, m_ref, qkvt_ref, w_ref, qkvb_ref, ub_ref, vec_ref, *rest
):
    if save:
        (z2_ref, qkvm_ref, pm_ref, am_ref, z1b_ref, g_ref, gp_ref, xh1_ref, xh2_ref, inv_ref) = rest[:10]
        wv, qkv, sem, sem2 = rest[10:]
    else:
        z2_ref = rest[0]
        wv, qkv, sem, sem2 = rest[1:]
    nb = w_ref.shape[0]
    d = w_ref.shape[1]
    seg = qkvt_ref.shape[1]
    mp = m_ref.shape[0]
    w1 = HPB * HD
    tokcopy = pltpu.make_async_copy(qkvt_ref, qkv.at[:, 0:seg, :], sem2)
    tokcopy.start()
    copies = load_w(w_ref, wv, sem)
    mem = m_ref[...]
    mb = mem.astype(BF)
    tokcopy.wait()
    out = jnp.zeros((mp, d), F32)
    keep = lax.broadcasted_iota(jnp.int32, (mp, seg + mp), 1) < seg + nmem
    for j in range(nb):
        copies[0, j].wait()
        acc = nn(mb, wv[j, :, 0 : 3 * w1]) + qkvb_ref[j]
        qkv[j, seg : seg + mp, 0:w1] = (acc[:, 0:w1].astype(BF) * 0.125).astype(BF)
        qkv[j, seg : seg + mp, w1 : 3 * w1] = acc[:, w1 : 3 * w1].astype(BF)
        parts = [jnp.zeros((mp, HD), F32)]
        for i in range(HPB):
            q = qkv[j, seg : seg + mp, i * HD : (i + 1) * HD]
            k = qkv[j, :, w1 + i * HD : w1 + (i + 1) * HD]
            v = qkv[j, :, 2 * w1 + i * HD : 2 * w1 + (i + 1) * HD]
            s = jnp.where(keep, nt(q, k), NEG)
            e = jnp.exp(s - jnp.max(s, axis=-1, keepdims=True))
            p = (e / jnp.sum(e, axis=-1, keepdims=True)).astype(BF)
            if save:
                pm_ref[j * HPB + i] = p
            parts.append(nn(p, v))
        a = jnp.concatenate(parts, axis=1).astype(BF)
        if save:
            am_ref[j] = a
        out += nt(a, wv[j, :, d - 4 * HD : d])
    xh1, inv1 = norm_stats(mem + out + vec_ref[0:1])
    z1 = xh1 * vec_ref[1:2] + vec_ref[2:3]
    z1b = z1.astype(BF)
    y = jnp.zeros((mp, d), F32)
    for j in range(nb):
        copies[1, j].wait()
        copies[2, j].wait()
        f = nn(z1b, wv[j, :, d : 2 * d]) + ub_ref[j]
        g, gp = gelu_both(f)
        g = g.astype(BF)
        if save:
            g_ref[j] = g
            gp_ref[j] = gp
        y += nt(g, wv[j, :, 2 * d : 3 * d])
    xh2, inv2 = norm_stats(z1 + y + vec_ref[3:4])
    z2 = xh2 * vec_ref[4:5] + vec_ref[5:6]
    z2_ref[...] = jnp.where(rows_mask((mp, d), nmem), z2, 0.0)
    if save:
        qkvm_ref[...] = qkv[:, seg : seg + mp, :]
        z1b_ref[...] = z1b
        xh1_ref[...] = xh1
        xh2_ref[...] = xh2
        inv_ref[:, 0:128] = jnp.broadcast_to(inv1, (mp, 128))
        inv_ref[:, 128:256] = jnp.broadcast_to(inv2, (mp, 128))


def mem_forward(m, qkvt, w, qkvb, ub, vec, nmem, save):
    nb, d, _ = w.shape
    seg = qkvt.shape[1]
    mp = m.shape[0]
    sds = jax.ShapeDtypeStruct
    shapes = [sds((mp, d), F32)]
    if save:
        shapes += [
            sds((nb, mp, 3 * HPB * HD), BF),
            sds((nb * HPB, mp, seg + mp), BF),
            sds((nb, mp, 4 * HD), BF),
            sds((mp, d), BF),
            sds((nb, mp, d), BF),
            sds((nb, mp, d), F32),
            sds((mp, d), F32),
            sds((mp, d), F32),
            sds((mp, 256), F32),
        ]
    return pl.pallas_call(
        functools.partial(mem_forward_kernel, nmem, save),
        out_shape=shapes,
        in_specs=[vm_spec(), any_spec(), any_spec(), vm_spec(), vm_spec(), vm_spec()],
        out_specs=[vm_spec()] * len(shapes),
        scratch_shapes=[
            pltpu.VMEM((nb, d, 3 * d), BF),
            pltpu.VMEM((nb, seg + mp, 3 * HPB * HD), BF),
            pltpu.SemaphoreType.DMA((3, nb)),
            pltpu.SemaphoreType.DMA,
        ],
        compiler_params=params(),
        cost_estimate=pl.CostEstimate(
            flops=2 * mp * d * d * 12, bytes_accessed=24 * d * d, transcendentals=0
        ),
        name="mem_forward",
    )(m, qkvt, w, qkvb, ub, vec)


def colsum(x):
    return jnp.sum(x, axis=0, keepdims=True)


CH = 64


def token_kernel(
    nmem,
    tok_ref,
    ct_ref,
    live_ref,
    m_ref,
    qkvt_ref,
    w_ref,
    qkvb_ref,
    ub_ref,
    vec_ref,
    out_ref,
    z1b_ref,
    a_ref,
    g_ref,
    gf_ref,
    gr2b_ref,
    gr1_ref,
    gq_ref,
    gkv_ref,
    base_ref,
    small_ref,
    ubg_ref,
    wv,
    qkv,
    probs,
    big,
    one,
    xh1,
    xh2,
    inv,
    gp,
    sem,
    sem2,
):
    nb, d, _ = w_ref.shape
    seg = tok_ref.shape[0]
    mp = m_ref.shape[0]
    keys = seg + mp
    w1 = HPB * HD
    steps = seg // CH
    tokcopy = pltpu.make_async_copy(qkvt_ref, qkv.at[:, 0:seg, :], sem2)
    tokcopy.start()
    copies = load_w(w_ref, wv, sem)
    mb = m_ref[...].astype(BF)
    for j in range(nb):
        copies[0, j].wait()
        acc = nn(mb, wv[j, :, 0 : 3 * w1]) + qkvb_ref[j]
        qkv[j, seg:keys, 0:w1] = (acc[:, 0:w1].astype(BF) * 0.125).astype(BF)
        qkv[j, seg:keys, w1 : 3 * w1] = acc[:, w1 : 3 * w1].astype(BF)
    tokcopy.wait()
    one[...] = jnp.zeros_like(one)
    tail = seg + (nmem // 8) * 8

    def attend(j, _):
        vt = qkv[j, :, 2 * w1 : 3 * w1].astype(F32).T.astype(BF)
        parts = [jnp.zeros((HD, seg), F32)]
        for i in range(HPB):
            q = qkv[j, 0:seg, i * HD : (i + 1) * HD]
            k = qkv[j, :, w1 + i * HD : w1 + (i + 1) * HD]
            big[0:keys, 0:seg] = nt(k, q)
            big[tail:keys, 0:seg] = jnp.where(
                rows_mask((keys - tail, seg), seg + nmem - tail), big[tail:keys, 0:seg], NEG
            )
            for c in range(seg // 128):
                cols = slice(c * 128, (c + 1) * 128)
                s = big[0:keys, cols]
                e = jnp.exp(s - jnp.max(s, axis=0, keepdims=True))
                p = e * (1.0 / jnp.sum(e, axis=0, keepdims=True))
                probs[j * HPB + i, :, cols] = p.astype(BF)
            parts.append(nn(vt[i * HD : (i + 1) * HD], probs[j * HPB + i]))
        a = jnp.concatenate(parts, axis=0).T.astype(BF)
        a_ref[j] = a
        one[...] += nt(a, wv[j, :, d - 4 * HD : d])
        return 0

    lax.fori_loop(0, nb, attend, 0)

    def first(c, _):
        rows = pl.ds(pl.multiple_of(c * CH, CH), CH)
        r = tok_ref[rows, :].astype(F32) + one[rows, :] + vec_ref[0:1]
        x, v = norm_stats(r)
        xh1[rows, :] = x
        inv[rows, 0:128] = jnp.broadcast_to(v, (CH, 128))
        z1 = x * vec_ref[1:2] + vec_ref[2:3]
        z1b_ref[rows, :] = z1.astype(BF)
        one[rows, :] = z1 + vec_ref[3:4]
        return 0

    lax.fori_loop(0, steps, first, 0)
    for part in (1, 2):
        for j in range(nb):
            copies[part, j].wait()

    def feed(j, _):
        big[0:seg, 0:d] = nn(z1b_ref[...], wv[j, :, d : 2 * d])

        def act(c, _):
            rows = pl.ds(pl.multiple_of(c * 32, 32), 32)
            g, p = gelu_both(big[rows, 0:d] + ub_ref[j])
            g_ref[j, rows, :] = g.astype(BF)
            gp[j, rows, :] = p.astype(BF)
            return 0

        lax.fori_loop(0, seg // 32, act, 0)
        one[...] += nt(g_ref[j], wv[j, :, 2 * d : 3 * d])
        return 0

    lax.fori_loop(0, nb, feed, 0)
    zero = jnp.zeros((1, d), F32)

    def second(c, carry):
        sg, ss, sb = carry
        rows = pl.ds(pl.multiple_of(c * CH, CH), CH)
        x, v = norm_stats(one[rows, :])
        out_ref[rows, :] = ((x * vec_ref[4:5] + vec_ref[5:6]) * live_ref[0:1, 0:1]).astype(BF)
        gz = ct_ref[rows, :].astype(F32) * live_ref[0:1, 0:1]
        gr = norm_back(gz * vec_ref[4:5], x, v)
        one[rows, :] = gr
        gr2b_ref[rows, :] = gr.astype(BF)
        return (sg + colsum(gz * x), ss + colsum(gz), sb + colsum(gr))

    sg, ss, sb = lax.fori_loop(0, steps, second, (zero, zero, zero))
    small_ref[3:4] = sb
    small_ref[4:5] = sg
    small_ref[5:6] = ss

    def feed_back(j, _):
        big[0:seg, 0:d] = nn(gr2b_ref[...], wv[j, :, 2 * d : 3 * d])

        def act(c, total):
            rows = pl.ds(pl.multiple_of(c * CH, CH), CH)
            gf = (big[rows, 0:d] * gp[j, rows, :].astype(F32)).astype(BF)
            gf_ref[j, rows, :] = gf
            return total + colsum(gf.astype(F32))

        ubg_ref[j] = lax.fori_loop(0, steps, act, zero)
        one[...] += nt(gf_ref[j], wv[j, :, d : 2 * d])
        return 0

    lax.fori_loop(0, nb, feed_back, 0)

    def first_back(c, carry):
        sg, ss, sb = carry
        rows = pl.ds(pl.multiple_of(c * CH, CH), CH)
        gz = one[rows, :]
        x = xh1[rows, :]
        gr = norm_back(gz * vec_ref[1:2], x, inv[rows, 0:1])
        gr1_ref[rows, :] = gr
        xh2[rows, :] = gr.astype(BF)
        return (sg + colsum(gz * x), ss + colsum(gz), sb + colsum(gr))

    sg, ss, sb = lax.fori_loop(0, steps, first_back, (zero, zero, zero))
    small_ref[0:1] = sb
    small_ref[1:2] = sg
    small_ref[2:3] = ss
    small_ref[6:8] = jnp.zeros((2, d), F32)

    def attend_back(j, base):
        ga = nn(xh2[...], wv[j, :, d - 4 * HD : d])
        gab = ga.astype(BF)
        delta = (gab.astype(F32) * a_ref[j].astype(F32)).T
        kt = qkv[j, :, w1 : 2 * w1].astype(F32).T.astype(BF)
        gqs = []
        gks = []
        gvs = []
        for i in range(HPB):
            q = qkv[j, 0:seg, i * HD : (i + 1) * HD]
            v = qkv[j, :, 2 * w1 + i * HD : 2 * w1 + (i + 1) * HD]
            g = gab[:, (i + 1) * HD : (i + 2) * HD]
            p = probs[j * HPB + i]
            dl = jnp.sum(delta[(i + 1) * HD : (i + 2) * HD], axis=0, keepdims=True)
            gvs.append(nn(p, g))
            gs = (p.astype(F32) * (nt(v, g) - dl)).astype(BF)
            gks.append(nn(gs, q))
            gqs.append(nn(kt[i * HD : (i + 1) * HD], gs))
        gq_ref[j] = (jnp.concatenate(gqs, axis=0).T * 0.125).astype(BF)
        gkv = jnp.concatenate(gks + gvs, axis=1)
        gkv_ref[j] = gkv
        gm = jnp.concatenate([jnp.zeros((mp, w1), F32), gkv[seg:keys]], axis=1).astype(BF)
        return base + nt(gm, wv[j, :, 0 : 3 * w1])

    base_ref[...] = lax.fori_loop(0, nb, attend_back, jnp.zeros((mp, d), F32))


def token_call(tok, ct, live, m, qkvt, w, qkvb, ub, vec, nmem):
    nb, d, _ = w.shape
    seg = tok.shape[0]
    mp = m.shape[0]
    keys = seg + mp
    w1 = HPB * HD
    sds = jax.ShapeDtypeStruct
    shapes = [
        sds((seg, d), BF),
        sds((seg, d), BF),
        sds((nb, seg, 4 * HD), BF),
        sds((nb, seg, d), BF),
        sds((nb, seg, d), BF),
        sds((seg, d), BF),
        sds((seg, d), F32),
        sds((nb, seg, w1), BF),
        sds((nb, keys, 2 * w1), F32),
        sds((mp, d), F32),
        sds((8, d), F32),
        sds((nb, 1, d), F32),
    ]
    return pl.pallas_call(
        functools.partial(token_kernel, nmem),
        out_shape=shapes,
        in_specs=[vm_spec()] * 4 + [any_spec()] * 2 + [vm_spec()] * 3,
        out_specs=[vm_spec()] * len(shapes),
        scratch_shapes=[
            pltpu.VMEM((nb, d, 3 * d), BF),
            pltpu.VMEM((nb, keys, 3 * w1), BF),
            pltpu.VMEM((nb * HPB, keys, seg), BF),
            pltpu.VMEM((keys, d), F32),
            pltpu.VMEM((seg, d), F32),
            pltpu.VMEM((seg, d), F32),
            pltpu.VMEM((seg, d), BF),
            pltpu.VMEM((seg, 128), F32),
            pltpu.VMEM((nb, seg, d), BF),
            pltpu.SemaphoreType.DMA((3, nb)),
            pltpu.SemaphoreType.DMA,
        ],
        compiler_params=params(),
        cost_estimate=pl.CostEstimate(
            flops=5 * seg * d * d * 12, bytes_accessed=60 * d * d, transcendentals=0
        ),
        name="token_rows",
    )(tok, ct, live, m, qkvt, w, qkvb, ub, vec)


def mem_backward_kernel(nmem, full, *refs):
    refs = list(refs)
    (g_ref, qkvt_ref, w_ref, vec_ref, base_ref, qkvm_ref, pm_ref, am_ref, gp_ref, xh1_ref, xh2_ref, inv_ref) = refs[:12]
    refs = refs[12:]
    if full:
        (gq_ref, gkv_ref, gr1t_ref) = refs[:3]
        (gm_ref, gr2b_ref, gf_ref, gr1b_ref, gqkv_ref, ig_ref, small_ref, ubg_ref, qvb_ref) = refs[3:12]
        wv, qkv, one, sem, sem2 = refs[12:]
    else:
        gm_ref = refs[0]
        wv, qkv, sem, sem2 = refs[1:]
    nb, d, _ = w_ref.shape
    seg = qkvt_ref.shape[1]
    mp = g_ref.shape[0]
    keys = seg + mp
    w1 = HPB * HD
    tokcopy = pltpu.make_async_copy(qkvt_ref, qkv.at[:, 0:seg, :], sem2)
    tokcopy.start()
    copies = load_w(w_ref, wv, sem)
    qkv[:, seg:keys, :] = qkvm_ref[...]
    gz = g_ref[...]
    xh2 = xh2_ref[...]
    gr2 = norm_back(gz * vec_ref[4:5], xh2, inv_ref[:, 128:129])
    gr2b = gr2.astype(BF)
    acc = gr2
    for j in range(nb):
        copies[2, j].wait()
        copies[1, j].wait()
        gf = (nn(gr2b, wv[j, :, 2 * d : 3 * d]) * gp_ref[j]).astype(BF)
        if full:
            gf_ref[j] = gf
            ubg_ref[j] = colsum(gf.astype(F32))
        acc += nt(gf, wv[j, :, d : 2 * d])
    xh1 = xh1_ref[...]
    gr1 = norm_back(acc * vec_ref[1:2], xh1, inv_ref[:, 0:1])
    gr1b = gr1.astype(BF)
    if full:
        small_ref[0:1] = colsum(gr1)
        small_ref[1:2] = colsum(acc * xh1)
        small_ref[2:3] = colsum(acc)
        small_ref[3:4] = colsum(gr2)
        small_ref[4:5] = colsum(gz * xh2)
        small_ref[5:6] = colsum(gz)
        small_ref[6:8] = jnp.zeros((2, d), F32)
        gr2b_ref[...] = gr2b
        gr1b_ref[...] = gr1b
        one[...] = gr1t_ref[...]
    tokcopy.wait()
    out = gr1 if full else gr1 + base_ref[...]
    for j in range(nb):
        copies[0, j].wait()
        gab = nn(gr1b, wv[j, :, d - 4 * HD : d]).astype(BF)
        prod = gab.astype(F32) * am_ref[j].astype(F32)
        gqs = []
        gks = []
        gvs = []
        for i in range(HPB):
            q = qkv[j, seg:keys, i * HD : (i + 1) * HD]
            k = qkv[j, :, w1 + i * HD : w1 + (i + 1) * HD]
            v = qkv[j, :, 2 * w1 + i * HD : 2 * w1 + (i + 1) * HD]
            g = gab[:, (i + 1) * HD : (i + 2) * HD]
            p = pm_ref[j * HPB + i]
            pf = p.astype(F32)
            dl = jnp.sum(prod[:, (i + 1) * HD : (i + 2) * HD], axis=1, keepdims=True)
            gs = pf * (nt(g, v) - dl)
            gsb = gs.astype(BF)
            gqs.append(nn(gsb, k) * 0.125)
            if full:
                gks.append(nn(gsb.astype(F32).T.astype(BF), q))
                gvs.append(nn(pf.T.astype(BF), g))
            else:
                gks.append(nn(gsb[:, seg:keys].astype(F32).T.astype(BF), q))
                gvs.append(nn(pf[:, seg:keys].T.astype(BF), g))
        gq = jnp.concatenate(gqs, axis=1)
        gkv = jnp.concatenate(gks + gvs, axis=1)
        if full:
            gkv = gkv + gkv_ref[j]
            gqkv_ref[j, 0:seg, 0:w1] = gq_ref[j]
            gqkv_ref[j, seg:keys, 0:w1] = gq.astype(BF)
            gkvb = gkv.astype(BF)
            gqkv_ref[j, :, w1 : 3 * w1] = gkvb
            qvb_ref[j, :, 0 : 3 * w1] = jnp.concatenate(
                [
                    colsum(gq_ref[j].astype(F32)) + colsum(gq.astype(BF).astype(F32)),
                    colsum(gkvb.astype(F32)),
                ],
                axis=1,
            )
            one[...] += nt(gqkv_ref[j, 0:seg, :], wv[j, :, 0 : 3 * w1])
            out += nt(gqkv_ref[j, seg:keys, :], wv[j, :, 0 : 3 * w1])
        else:
            gm = jnp.concatenate([gq, gkv], axis=1).astype(BF)
            out += nt(gm, wv[j, :, 0 : 3 * w1])
    gm_ref[...] = out
    if full:
        ig_ref[...] = one[...].astype(BF)


def mem_backward(g, qkvt, w, vec, base, saved, nmem, extra=None):
    full = extra is not None
    nb, d, _ = w.shape
    seg = qkvt.shape[1]
    mp = g.shape[0]
    keys = seg + mp
    w1 = HPB * HD
    qkvm, pm, am, z1b, _, gp, xh1, xh2, inv = saved
    sds = jax.ShapeDtypeStruct
    shapes = [sds((mp, d), F32)]
    args = [g, qkvt, w, vec, base, qkvm, pm, am, gp, xh1, xh2, inv]
    specs = [vm_spec(), any_spec(), any_spec()] + [vm_spec()] * 9
    scratch = [
        pltpu.VMEM((nb, d, 3 * d), BF),
        pltpu.VMEM((nb, keys, 3 * w1), BF),
    ]
    if full:
        args += list(extra)
        specs += [vm_spec()] * 3
        shapes += [
            sds((mp, d), BF),
            sds((nb, mp, d), BF),
            sds((mp, d), BF),
            sds((nb, keys, 3 * w1), BF),
            sds((seg, d), BF),
            sds((8, d), F32),
            sds((nb, 1, d), F32),
            sds((nb, 1, 3 * w1), F32),
        ]
        scratch += [pltpu.VMEM((seg, d), F32)]
    scratch += [pltpu.SemaphoreType.DMA((3, nb)), pltpu.SemaphoreType.DMA]
    return pl.pallas_call(
        functools.partial(mem_backward_kernel, nmem, full),
        out_shape=shapes,
        in_specs=specs,
        out_specs=[vm_spec()] * len(shapes),
        scratch_shapes=scratch,
        compiler_params=params(),
        cost_estimate=pl.CostEstimate(
            flops=2 * mp * d * d * 12, bytes_accessed=24 * d * d, transcendentals=0
        ),
        name="mem_backward_full" if full else "mem_backward",
    )(*args)


def weight_grad_kernel(
    tok_ref, m_ref, gqkv_ref, gr1_ref, gr1m_ref, a_ref, am_ref, z1b_ref, z1m_ref, gf_ref, gfm_ref,
    gr2b_ref, gr2m_ref, g_ref, gm_ref, out_ref, lt
):
    seg, d = tok_ref.shape
    mp = m_ref.shape[0]
    keys = seg + mp
    w1 = HPB * HD

    @pl.when(pl.program_id(0) == 0)
    def _():
        pairs = (
            (tok_ref, m_ref),
            (gr1_ref, gr1m_ref),
            (z1b_ref, z1m_ref),
            (gr2b_ref, gr2m_ref),
        )
        for t, (a, b) in enumerate(pairs):
            lt[t, :, 0:seg] = a[...].astype(F32).T.astype(BF)
            lt[t, :, seg:keys] = b[...].astype(BF).astype(F32).T.astype(BF)

    out_ref[0, :, 0 : 3 * w1] = nn(lt[0], gqkv_ref[0]).astype(BF)
    go = nn(lt[1, :, 0:seg], a_ref[0]) + nn(lt[1, :, seg:keys], am_ref[0])
    out_ref[0, :, 3 * w1 : d] = go[:, HD : HD + w1].astype(BF)
    up = nn(lt[2, :, 0:seg], gf_ref[0]) + nn(lt[2, :, seg:keys], gfm_ref[0])
    out_ref[0, :, d : 2 * d] = up.astype(BF)
    dn = nn(lt[3, :, 0:seg], g_ref[0]) + nn(lt[3, :, seg:keys], gm_ref[0])
    out_ref[0, :, 2 * d : 3 * d] = dn.astype(BF)


def weight_grad(tok, m, gqkv, gr1, gr1m, a, am, z1b, z1m, gf, gfm, gr2b, gr2m, g, gm):
    seg, d = tok.shape
    mp = m.shape[0]
    nb = g.shape[0]
    args = (tok, m, gqkv, gr1, gr1m, a, am, z1b, z1m, gf, gfm, gr2b, gr2m, g, gm)
    specs = []
    for x in args:
        if x.ndim == 2:
            specs.append(pl.BlockSpec(x.shape, lambda j: (0, 0)))
        else:
            specs.append(pl.BlockSpec((1,) + x.shape[1:], lambda j: (j, 0, 0)))
    return pl.pallas_call(
        weight_grad_kernel,
        grid=(nb,),
        out_shape=jax.ShapeDtypeStruct((nb, d, 3 * d), BF),
        in_specs=specs,
        out_specs=pl.BlockSpec((1, d, 3 * d), lambda j: (j, 0, 0)),
        scratch_shapes=[pltpu.VMEM((4, d, seg + mp), BF)],
        compiler_params=params(),
        cost_estimate=pl.CostEstimate(
            flops=2 * seg * d * d * 12, bytes_accessed=48 * d * d, transcendentals=0
        ),
        name="weight_grad",
    )(*args)


def body(
    tokens, memory_init, query_weight, query_bias, key_weight, value_weight, value_bias, out_weight,
    out_bias, first_gain, first_shift, up_weight, up_bias, down_weight, down_bias, second_gain,
    second_shift, cotangent, group_segs, chain_group
):
    nd = lax.axis_size("dp")
    nb = lax.axis_size("mp")
    me = lax.axis_index("mp")
    segments = tokens.shape[1]
    d = tokens.shape[3]
    part = tokens.shape[2]
    seg = part * nb
    nmem = memory_init.shape[0] * nb
    pad = -(-nmem // 16) * 16
    both = ("mp", "dp")
    wl = jnp.concatenate(
        [query_weight, key_weight, value_weight, out_weight.T, up_weight, down_weight.T], axis=1
    )
    w = lax.all_gather(wl, both, axis=0).reshape(nb, d, 3 * d)
    vecs = (out_bias, first_gain, first_shift, down_bias, second_gain, second_shift)
    small = jnp.concatenate(
        (query_bias, value_bias, up_bias) + vecs + (memory_init.reshape(-1),)
    )
    n1 = query_bias.shape[0]
    n2 = up_bias.shape[0]
    sg = lax.all_gather(small, both, axis=0).reshape(nb, nd, -1)
    qb = sg[:, :, 0:n1].reshape(nb, 1, -1).astype(F32)
    vb = sg[:, :, n1 : 2 * n1].reshape(nb, 1, -1).astype(F32)
    qkvb = jnp.concatenate([qb, jnp.zeros_like(qb), vb], axis=2)
    ub = sg[:, :, 2 * n1 : 2 * n1 + n2].reshape(nb, 1, -1).astype(F32)
    at = 2 * n1 + n2
    vec = sg[:, :, at : at + 6 * n1].reshape(nb, nd, 6, n1).transpose(2, 1, 0, 3).reshape(6, d)
    vec = jnp.pad(vec.astype(F32), ((0, 2), (0, 0)))
    ml = memory_init.shape[0]
    m0 = sg[:, :, at + 6 * n1 :].reshape(nb, nd, ml, -1).transpose(0, 2, 1, 3).reshape(nmem, d)
    m0 = jnp.pad(m0.astype(F32), ((0, pad - nmem), (0, 0)))
    tok = lax.all_to_all(tokens[0], "mp", 0, 1, tiled=True).reshape(seg, d)
    ct = lax.all_to_all(cotangent[0], "mp", 0, 1, tiled=True).reshape(seg, d)
    match = chain_group[:, None] == jnp.arange(group_segs.shape[0], dtype=jnp.int32)[None, :]
    count = jnp.sum(jnp.where(match, group_segs[None, :], 0))
    live = (me < count).astype(F32)
    live2 = jnp.full((8, 128), live, F32)
    qkvt = qkv_call(tok, w, qkvb)
    m = jnp.where(me == 0, m0, 0.0)
    own = m
    for s in range(segments - 1):
        (z,) = mem_forward(m, qkvt, w, qkvb, ub, vec, nmem, False)
        m = lax.ppermute(z, "mp", [(s, s + 1)])
        own = own + m
    (out, z1b, a, g, gf, gr2b, gr1, gq, gkv, base, sm, ubg) = token_call(
        tok, ct, live2, own, qkvt, w, qkvb, ub, vec, nmem
    )
    z2m, *saved = mem_forward(own, qkvt, w, qkvb, ub, vec, nmem, True)
    send = base
    gin = jnp.zeros_like(base)
    gw = None
    for s in reversed(range(segments - 1)):
        recv = lax.ppermute(send, "mp", [(s + 1, s)])
        gin = gin + recv
        if s > 0:
            (send,) = mem_backward(recv, qkvt, w, vec, base, saved, nmem)
    gm, gr2m, gfm, gr1m, gqkv, ig, smm, ubgm, qvb = mem_backward(
        gin, qkvt, w, vec, base, saved, nmem, (gq, gkv, gr1)
    )
    qkvm, pm, am, z1m, g_m, gp_m, xh1, xh2, inv = saved
    wg = weight_grad(
        tok, own, gqkv, gr1.astype(BF), gr1m, a, am, z1b, z1m, gf, gfm, gr2b, gr2m, g, g_m
    )
    wg = lax.psum_scatter(
        wg.reshape(nb * nd, d // nd, 3 * d), both, scatter_dimension=0, tiled=False
    ).astype(F32)
    chains = nd * tokens.shape[0]
    norm = live * jnp.sum(z2m * z2m) / (nmem * d * chains)
    norms = jnp.where(jnp.arange(segments) == me, norm, 0.0)
    w1 = d // nb
    smt = (sm + smm)[0:6].reshape(6, nd, nb, n1).transpose(2, 1, 0, 3).reshape(nb, nd, 6 * n1)
    qbg = qvb[:, 0, 0:w1].reshape(nb, nd, n1)
    vbg = qvb[:, 0, 2 * w1 : 3 * w1].reshape(nb, nd, n1)
    ubt = (ubg + ubgm).reshape(nb, nd, n2)
    gmi = jnp.where(me == 0, gm[0:nmem], 0.0).reshape(nb, ml, nd, d // nd).transpose(0, 2, 1, 3)
    smalls = jnp.concatenate(
        [
            qbg, vbg, ubt, smt, gmi.reshape(nb, nd, -1),
            jnp.broadcast_to(norms, (nb, nd, segments)),
        ],
        axis=2,
    ).reshape(nb * nd, -1)
    sr = lax.psum_scatter(smalls, both, scatter_dimension=0, tiled=False)
    vg = sr[at : at + 6 * n1].reshape(6, n1)
    layer_out = lax.all_to_all(out.reshape(nb, part, d), "mp", 0, 0, tiled=True)
    input_grad = lax.all_to_all(ig.reshape(nb, part, d), "mp", 0, 0, tiled=True)
    return (
        layer_out[None],
        input_grad[None],
        sr[at + 6 * n1 : at + 6 * n1 + ml * (d // nd)].reshape(ml, d // nd),
        wg[:, 0:w1],
        sr[0:n1],
        wg[:, w1 : 2 * w1],
        wg[:, 2 * w1 : 3 * w1],
        sr[n1 : 2 * n1],
        wg[:, 3 * w1 : d].T,
        vg[0],
        vg[1],
        vg[2],
        wg[:, d : 2 * d],
        sr[2 * n1 : at],
        wg[:, 2 * d : 3 * d].T,
        vg[3],
        vg[4],
        vg[5],
        sr[at + 6 * n1 + ml * (d // nd) :],
    )


def solution(mesh):
    rows = P("dp", None, "mp", None)
    md, dm = P(("mp", "dp")), P(("dp", "mp"))
    win, wout = P("dp", "mp"), P("mp", "dp")
    in_specs = (
        rows, wout, win, md, win, win, md, wout, dm, dm, dm, win, md, wout, dm, dm, dm, rows, P(),
        P("dp"),
    )
    out_specs = (
        rows, rows, wout, win, md, win, win, md, wout, dm, dm, dm, win, md, wout, dm, dm, dm, P(),
    )
    return jax.shard_map(body, mesh=mesh, in_specs=in_specs, out_specs=out_specs, check_vma=False)
```

time: 1520 us -> 652 us (0.43)
  blocking collectives: 626 us -> 86 us
  Pallas kernels: 0 us -> 208 us
  waiting for transfers between devices: 445 us -> 273 us
  matrix products: 146 us -> 0 us
  local copies, waits for them, and re-layouts: 106 us -> 30.9 us
  starting transfers between devices: 80.6 us -> 18.9 us
  other arithmetic: 70.5 us -> 10.8 us
    all_gather x37 -> x1, blocking collectives: 383 us -> 71.8 us  [body(): sg = lax.all_gather(small, both, axis=0).reshape(nb, nd, -1)]
    reduce_scatter x21 -> x1, waiting for transfers between devices: 415 us -> 161 us  [body(): lax.psum_scatter(wg.reshape(nb * nd, d // nd, 3 * d), both, scatter_dimen...]
    unnamed x20 -> x0, blocking collectives: 243 us -> none
    pallas_call x0 -> x10, Pallas kernels: none -> 208 us  [the longest x4 69.9 us: mem_forward(): pl.pallas_call(functools.partial(mem_forward_kernel, nmem, save), out_sha...]
    dot_general x96 -> x0, matrix products: 146 us -> none  [the longest x24 33.2 us: contract_rows(): lax.dot_general(left, right, (((0,), (0,)), ((), ())), preferred_element_...]
    unnamed x34 -> x1, starting transfers between devices: 79.2 us -> 0.57 us
    unnamed x744 -> x37, local copies, waits for them, and re-layouts: 75.2 us -> 7.93 us
    unnamed x59 -> x4, waiting for transfers between devices: 26.8 us -> 79.8 us
  transfers between devices with their start and end apart: 57 -> 12, of which waited for: 26 -> 4; matrix products, arithmetic and copies ran while one was open for 15% -> 4% of each run, Pallas kernels for 0% -> 11%
where the time goes in v1:
time: 652 us; the launch traced here: 645 us
  waiting for transfers between devices  273 us (42%)
  Pallas kernels  208 us (32%)
  blocking collectives  86 us (13%)
  local copies, waits for them, and re-layouts  30.9 us (5%)
  starting transfers between devices  18.9 us (3%)
  between operations  16.6 us (3%)
  other arithmetic  10.8 us (2%)
    reduce_scatter x1, waiting for transfers between devices, body(): lax.psum_scatter(wg.reshape(nb * nd, d // nd, 3 * d), both, scatter_dimen...  161 us
    unnamed x4, waiting for transfers between devices  79.8 us
    all_gather x1, blocking collectives, body(): sg = lax.all_gather(small, both, axis=0).reshape(nb, nd, -1)  71.8 us
    pallas_call x4, Pallas kernels, mem_forward(): pl.pallas_call(functools.partial(mem_forward_kernel, nmem, save), out_sha...  69.9 us
    pallas_call x1, Pallas kernels, token_call(): pl.pallas_call(functools.partial(token_kernel, nmem), out_shape=shapes, i...  59.4 us
    pallas_call x3, Pallas kernels, mem_backward(): pl.pallas_call(functools.partial(mem_backward_kernel, nmem, full), out_sh...  51.8 us
    all_gather x1, waiting for transfers between devices, body(): w = lax.all_gather(wl, both, axis=0).reshape(nb, d, 3 * d)  22.3 us
    pallas_call x1, Pallas kernels, weight_grad(): pl.pallas_call(weight_grad_kernel, grid=(nb,), out_shape=jax.ShapeDtypeSt...  19.2 us
  transfers between devices with their start and end apart: 12, of which 4 were waited for; matrix products, arithmetic and copies ran while one was open for 4% of the time, Pallas kernels for 11%

profile of v1, /device:TPU:0, one launch (start us, length us, event | category | flops | bytes accessed | tf_op | source)
XLA Modules:
  0.0 644.7 jit_solution(16317262353247597627)
XLA Ops:
  8.1 1.9 concatenate.24
  10.1 4.2 all-to-all-start
  15.1 6.1 concatenate.23
  21.2 71.8 %all-gather.2 = bf16[32,1,768]{2,1,0:T(2,128)(2,1)S(1)} all-gather(bf16[1,1,768]{2,1,0:T(2,128)(2,1)S(1)} %reshape.200), channel_id=2, replica_groups=mesh['dp'=8,'mp'=4] {'mp','dp'}, dimensions={0}, use_global_device_ids=true | all-gather | bytes 50688 | tf_op jit(solution)/shard_map/all_gather | solution.py:676
  96.6 22.3 %all-gather.5.cloned.1.call-done = bf16[3072,2304]{1,0:T(8,128)(2,1)} async-done(((bf16[96,2304]{1,0:T(8,128)(2,1)}), bf16[3072,2304]{1,0:T(8,128)(2,1)}) %all-gather.5.cloned.1.call-update) | async-done | bytes 14155792 | tf_op jit(solution)/shard_map/all_gather | solution.py:669
  119.0 7.9 %qkv.1.qkvt_ref.refs_1_ = bf16[4,512,576]{2,1,0:T(8,128)(2,1)} custom-call(bf16[512,768]{1,0:T(8,128)(2,1)} %bitcast.65, bf16[4,768,2304]{2,1,0:T(8,128)(2,1)} %bitcast.55, f32[4,1,576]{2,1,0:T(1,128)} %pad_maximum_fusion.qkvb_ref), custom_call_target="tpu_custom_call" | custom-call | flops 1811939328 | bytes 4718592 | tf_op jit(solution)/shard_map/qkv/pallas_call | solution.py:80
  126.8 17.5 %mem_forward.4 = f32[32,768]{1,0:T(8,128)} custom-call(f32[32,768]{1,0:T(8,128)} %convert_select_fusion.m_ref, bf16[4,512,576]{2,1,0:T(8,128)(2,1)} %qkv.1.qkvt_ref.refs_1_, bf16[4,768,2304]{2,1,0:T(8,128)(2,1)} %bitcast.56, f32[4,1,576]{2,1,0:T(1,128)} %pad_maximum_fusion.qkvb_ref, f32[4,1,768]{2,1,0:T(1,128)} %reshape.194.ub_ref, ...), custom_call_target="tpu_custom_call" | custom-call | flops 452984832 | bytes 14155776 | tf_op jit(solution)/shard_map/mem_forward/pallas_call | solution.py:194
  144.3 2.2 collective-permute-start
  146.5 3.5 all-to-all-start.1
  151.2 17.5 %mem_forward.5 = f32[32,768]{1,0:T(8,128)} custom-call(f32[32,768]{1,0:T(8,128)} %copy-done.6, bf16[4,512,576]{2,1,0:T(8,128)(2,1)} %qkv.1.qkvt_ref.refs_1_, bf16[4,768,2304]{2,1,0:T(8,128)(2,1)} %bitcast.57, f32[4,1,576]{2,1,0:T(1,128)} %pad_maximum_fusion.qkvb_ref, f32[4,1,768]{2,1,0:T(1,128)} %reshape.194.ub_ref, f32[8,768]{1,0:T(8,128)} %pad_convert_fusion.vec_ref.refs_3_), custom_call_target="tpu_custom_call" | custom-call | flops 452984832 | bytes 14155776 | tf_op jit(solution)/shard_map/mem_forward/pallas_call | solution.py:194
  170.7 17.5 %mem_forward.6 = f32[32,768]{1,0:T(8,128)} custom-call(f32[32,768]{1,0:T(8,128)} %copy-done.9, bf16[4,512,576]{2,1,0:T(8,128)(2,1)} %qkv.1.qkvt_ref.refs_1_, bf16[4,768,2304]{2,1,0:T(8,128)(2,1)} %bitcast.58, f32[4,1,576]{2,1,0:T(1,128)} %pad_maximum_fusion.qkvb_ref, f32[4,1,768]{2,1,0:T(1,128)} %reshape.194.ub_ref, f32[8,768]{1,0:T(8,128)} %pad_convert_fusion.vec_ref.refs_3_), custom_call_target="tpu_custom_call" | custom-call | flops 452984832 | bytes 14155776 | tf_op jit(solution)/shard_map/mem_forward/pallas_call | solution.py:194
  192.8 59.4 %token_rows.1 = (bf16[512,768]{1,0:T(8,128)(2,1)}, bf16[512,768]{1,0:T(8,128)(2,1)}, bf16[4,512,256]{2,1,0:T(8,128)(2,1)}, bf16[4,512,768]{2,1,0:T(8,128)(2,1)},...) custom-call(bf16[512,768]{1,0:T(8,128)(2,1)} %bitcast.66, ...), custom_call_target="tpu_custom_call" | custom-call | flops 18119393280 | bytes 35389440 | tf_op jit(solution)/shard_map/token_rows/pallas_call | solution.py:426
  253.1 17.5 %mem_forward.7 = (f32[32,768]{1,0:T(8,128)}, bf16[4,32,576]{2,1,0:T(8,128)(2,1)}, bf16[12,32,544]{2,1,0:T(8,128)(2,1)}, bf16[4,32,256]{2,1,0:T(8,128)(2,1)}, bf1...) custom-call(f32[32,768]{1,0:T(8,128)} %add_add_fusion.1.m_ref, ...), custom_call_target="tpu_custom_call" | custom-call | flops 452984832 | bytes 14155776 | tf_op jit(solution)/shard_map/mem_forward/pallas_call | solution.py:194
  271.2 15.0 %mem_backward.2 = f32[32,768]{1,0:T(8,128)} custom-call(f32[32,768]{1,0:T(8,128)} %copy-done.4, bf16[4,512,576]{2,1,0:T(8,128)(2,1)} %qkv.1.qkvt_ref.refs_1_, bf16[4,768,2304]{2,1,0:T(8,128)(2,1)} %bitcast.61, f32[8,768]{1,0:T(8,128)} %pad_convert_fusion.vec_ref.refs_3_, f32[32,768]{1,0:T(8,128)} %get-tuple-element.51.refs_4_, ...), custom_call_target="tpu_custom_call" | custom-call | flops 452984832 | bytes 14155776 | tf_op jit(solution)/shard_map/mem_backward/pallas_call | solution.py:581
  289.8 14.9 %mem_backward.3 = f32[32,768]{1,0:T(8,128)} custom-call(f32[32,768]{1,0:T(8,128)} %copy-done.8, bf16[4,512,576]{2,1,0:T(8,128)(2,1)} %qkv.1.qkvt_ref.refs_1_, bf16[4,768,2304]{2,1,0:T(8,128)(2,1)} %bitcast.62, f32[8,768]{1,0:T(8,128)} %pad_convert_fusion.vec_ref.refs_3_, f32[32,768]{1,0:T(8,128)} %get-tuple-element.51.refs_4_, ...), custom_call_target="tpu_custom_call" | custom-call | flops 452984832 | bytes 14155776 | tf_op jit(solution)/shard_map/mem_backward/pallas_call | solution.py:581
  306.3 9.7 %collective-permute-done.5 = f32[32,768]{1,0:T(8,128)S(1)} collective-permute-done((f32[32,768]{1,0:T(8,128)}, f32[32,768]{1,0:T(8,128)S(1)}, u32[]{:S(2)}, u32[]{:S(2)}) %collective-permute-start.5) | collective-permute-done | bytes 98336 | tf_op jit(solution)/shard_map/ppermute | solution.py:708
  317.5 21.9 %mem_backward_full.1 = (f32[32,768]{1,0:T(8,128)}, bf16[32,768]{1,0:T(8,128)(2,1)}, bf16[4,32,768]{2,1,0:T(8,128)(2,1)}, bf16[32,768]{1,0:T(8,128)(2,1)}, bf16[4...) custom-call(f32[32,768]{1,0:T(8,128)} %add_add_fusion.refs_0_, ...), custom_call_target="tpu_custom_call" | custom-call | flops 452984832 | bytes 14155776 | tf_op jit(solution)/shard_map/mem_backward_full/pallas_call | solution.py:581
  344.4 19.2 %weight_grad.1 = bf16[4,768,2304]{2,1,0:T(8,128)(2,1)} custom-call(bf16[512,768]{1,0:T(8,128)(2,1)} %bitcast.67, f32[32,768]{1,0:T(8,128)} %add_add_fusion.1.m_ref, bf16[4,544,576]{2,1,0:T(8,128)(2,1)} %get-tuple-element.70.gqkv_ref, bf16[512,768]{1,0:T(8,128)(2,1)} %convert_element_type.82.gr1_ref, bf16[32,768]{1,0:T(8,128)(2,1)} %get-tuple-element.71.gr1m_ref, ...), custom_call_target="tpu_custom_call" | custom-call | flops 7247757312 | bytes 28311552 | tf_op jit(solution)/shard_map/weight_grad/pallas_call | solution.py:636
  364.8 14.2 %all_to_all.28 = bf16[4,128,768]{2,1,0:T(8,128)(2,1)S(1)} all-to-all(bf16[4,128,768]{2,1,0:T(8,128)(2,1)S(1)} %bitcast.71), channel_id=1, replica_groups=mesh['dp'=8,'mp'=4] {'mp'}, dimensions={0} | all-to-all | bytes 1572864 | tf_op jit(solution)/shard_map/all_to_all | solution.py:740
  379.0 3.5 all-to-all-start.3
  383.1 79.8 %all-reduce.5.cloned.1.call-done = f32[32,772]{1,0:T(8,128)} async-done(((f32[32,772]{1,0:T(8,128)}), f32[32,772]{1,0:T(8,128)}) %all-reduce.5.cloned.1.call-update) | async-done | bytes 98832
  465.0 1.9 dynamic-slice_bitcast_fusion.4
  468.9 2.2 dynamic-slice_bitcast_fusion.1
  471.1 161.4 %reduce-scatter.2.cloned.1.call-done = bf16[1,96,2304]{2,1,0:T(8,128)(2,1)} async-done(((bf16[32,96,2304]{2,1,0:T(8,128)(2,1)}), bf16[1,96,2304]{2,1,0:T(8,128)(2,1)}) %reduce-scatter.2.cloned.1.call-update) | async-done | bytes 442384 | tf_op jit(solution)/shard_map/reduce_scatter | solution.py:719
  (103 shorter events, 35.2 us)
Async XLA Ops:
  7.2 111.8 %all-gather.5.cloned.1.call-start = ((), (), s32[]{:S(2)}) async-start(), calls=%async_computation.6 | async-start | bytes 14598144 | tf_op jit(solution)/shard_map/all_gather | solution.py:669
  10.1 86.5 %all-to-all-start = ((bf16[4,128,768]{2,1,0:T(8,128)(2,1)}), bf16[4,128,768]{2,1,0:T(8,128)(2,1)S(1)}, u32[]{:S(2)}, u32[]{:S(2)}) async-start(bf16[4,128,768]{2,1,0:T(8,128)(2,1)} %bitcast.70), calls=%async_computation | async-start | bytes 1572864 | tf_op jit(solution)/shard_map/all_to_all | solution.py:687
  96.6 22.3 %copy-start = (bf16[4,128,768]{2,1,0:T(8,128)(2,1)}, bf16[4,128,768]{2,1,0:T(8,128)(2,1)S(1)}, u32[]{:S(2)}) copy-start(bf16[4,128,768]{2,1,0:T(8,128)(2,1)S(1)} %all-to-all-done) | copy-start | bytes 2359300
  144.3 6.3 collective-permute-start
  146.5 45.4 %all-to-all-start.1 = ((bf16[4,128,768]{2,1,0:T(8,128)(2,1)}), bf16[4,128,768]{2,1,0:T(8,128)(2,1)S(1)}, u32[]{:S(2)}, u32[]{:S(2)}) async-start(bf16[4,128,768]{2,1,0:T(8,128)(2,1)} %bitcast.2), calls=%async_computation.1 | async-start | bytes 1572864 | tf_op jit(solution)/shard_map/all_to_all | solution.py:688
  150.0 312.9 %all-reduce.5.cloned.1.call-start = ((), (), s32[]{:S(2)}) async-start(), calls=%async_computation.7 | async-start | bytes 229376
  150.6 0.6 copy-start.6
  168.7 1.3 collective-permute-start.1
  170.0 19.0 %copy-start.13 = (s32[6]{0:T(128)S(1)}, s32[6]{0:T(128)}, u32[]{:S(2)}) copy-start(s32[6]{0:T(128)} %param.38) | copy-start | bytes 76
  170.0 20.3 %copy-start.7 = (f32[32,768]{1,0:T(8,128)S(1)}, f32[32,768]{1,0:T(8,128)}, u32[]{:S(2)}) copy-start(f32[32,768]{1,0:T(8,128)} %copy-done.6) | copy-start | bytes 294916
  188.2 2.1 collective-permute-start.2
  191.9 0.9 copy-start.3
  252.2 18.4 %collective-permute-start.3 = (f32[32,768]{1,0:T(8,128)}, f32[32,768]{1,0:T(8,128)S(1)}, u32[]{:S(2)}, u32[]{:S(2)}) collective-permute-start(f32[32,768]{1,0:T(8,128)} %get-tuple-element.51.refs_4_), channel_id=1, source_target_pairs={{3,2},{7,6},{11,10},{15,14},{19,18},{23,22},{27,26},{31,30}} | collective-permute-start | bytes 294920 | tf_op jit(solution)/shard_map/ppermute | solution.py:708
  271.2 15.7 %copy-start.10 = (f32[32,768]{1,0:T(8,128)S(1)}, f32[32,768]{1,0:T(8,128)}, u32[]{:S(2)}) copy-start(f32[32,768]{1,0:T(8,128)} %get-tuple-element.69) | copy-start | bytes 294916
  271.2 17.0 %copy-start.1 = (f32[512,768]{1,0:T(8,128)S(1)}, f32[512,768]{1,0:T(8,128)}, u32[]{:S(2)}) copy-start(f32[512,768]{1,0:T(8,128)} %get-tuple-element.61.refs_14_) | copy-start | bytes 4718596
  286.2 2.9 collective-permute-start.4
  289.2 26.8 %copy-start.5 = (f32[32,768]{1,0:T(8,128)S(1)}, f32[32,768]{1,0:T(8,128)}, u32[]{:S(2)}) copy-start(f32[32,768]{1,0:T(8,128)} %copy-done.4) | copy-start | bytes 294916
  304.7 11.2 %collective-permute-start.5 = (f32[32,768]{1,0:T(8,128)}, f32[32,768]{1,0:T(8,128)S(1)}, u32[]{:S(2)}, u32[]{:S(2)}) collective-permute-start(f32[32,768]{1,0:T(8,128)} %mem_backward.3), channel_id=1, source_target_pairs={{1,0},{5,4},{9,8},{13,12},{17,16},{21,20},{25,24},{29,28}} | collective-permute-start | bytes 294920 | tf_op jit(solution)/shard_map/ppermute | solution.py:708
  317.5 21.9 %copy-start.12 = (f32[4,1,768]{2,1,0:T(1,128)S(1)}, f32[4,1,768]{2,1,0:T(1,128)}, u32[]{:S(2)}) copy-start(f32[4,1,768]{2,1,0:T(1,128)} %get-tuple-element.64) | copy-start | bytes 36868
  317.5 24.7 %copy-start.11 = (f32[8,768]{1,0:T(8,128)S(1)}, f32[8,768]{1,0:T(8,128)}, u32[]{:S(2)}) copy-start(f32[8,768]{1,0:T(8,128)} %get-tuple-element.66) | copy-start | bytes 73732
  344.1 288.3 %reduce-scatter.2.cloned.1.call-start = ((), (), s32[]{:S(2)}) async-start(), calls=%async_computation.5 | async-start | bytes 14598144 | tf_op jit(solution)/shard_map/reduce_scatter | solution.py:719
  363.6 1.1 copy-start.2
  363.7 18.8 %copy-start.14 = (u32[32]{0:T(128)S(1)}, u32[32]{0:T(128)}, u32[]{:S(2)}) copy-start(u32[32]{0:T(128)} %constant.34) | copy-start | bytes 388
  379.0 92.0 %all-to-all-start.3 = ((bf16[4,128,768]{2,1,0:T(8,128)(2,1)}), bf16[4,128,768]{2,1,0:T(8,128)(2,1)S(1)}, u32[]{:S(2)}, u32[]{:S(2)}) async-start(bf16[4,128,768]{2,1,0:T(8,128)(2,1)} %bitcast.12), calls=%async_computation.3 | async-start | bytes 1572864 | tf_op jit(solution)/shard_map/all_to_all | solution.py:741
  (3 other events, 1.9 us)
Sparse Core Ops, SparseCore 0:
  11.6 107.3 all-gather.4
  344.2 118.6 all-reduce.4
  468.9 163.4 reduce-scatter.1

commit v2 on v1

v2 whole, which is shorter than its diff:
```python
import functools

import jax
import jax.numpy as jnp
from jax import lax
from jax.experimental import pallas as pl
from jax.experimental.pallas import tpu as pltpu
from jax.sharding import PartitionSpec as P

HD = 64
HPB = 3
BF = jnp.bfloat16
F32 = jnp.float32
VMEM_LIMIT = 60 * 1024 * 1024
NEG = -1e30


def nn(a, b):
    return lax.dot_general(a, b, (((1,), (0,)), ((), ())), preferred_element_type=F32)


def nt(a, b):
    return lax.dot_general(a, b, (((1,), (1,)), ((), ())), preferred_element_type=F32)


def norm_stats(r):
    mean = jnp.mean(r, axis=-1, keepdims=True)
    c = r - mean
    inv = lax.rsqrt(jnp.mean(c * c, axis=-1, keepdims=True) + 1e-05)
    return c * inv, inv


def norm_back(g, xh, inv):
    return inv * (
        g - jnp.mean(g, axis=-1, keepdims=True) - xh * jnp.mean(g * xh, axis=-1, keepdims=True)
    )


def gelu_both(f):
    cdf = 0.5 + 0.5 * lax.erf(f * (0.5**0.5))
    pdf = jnp.exp(-0.5 * f * f) * ((2.0 * jnp.pi) ** -0.5)
    return f * cdf, cdf + f * pdf


def rows_mask(shape, count):
    return lax.broadcasted_iota(jnp.int32, shape, 0) < count


def any_spec():
    return pl.BlockSpec(memory_space=pl.ANY)


def vm_spec():
    return pl.BlockSpec(memory_space=pltpu.VMEM)


def params():
    return pltpu.CompilerParams(vmem_limit_bytes=VMEM_LIMIT)


def sm_spec():
    return pl.BlockSpec(memory_space=pltpu.SMEM)


class Weights:
    def __init__(self, me, w_ref, wv, sem, order, depth=4):
        d = w_ref.shape[1]
        self.copies = []
        self.place = {}
        for n, (part, j) in enumerate(order):
            cols = slice(part * d, (part + 1) * d)
            self.place[part, j] = n
            self.copies.append(
                pltpu.make_async_copy(w_ref.at[j ^ me, :, cols], wv.at[j, :, cols], sem.at[n])
            )
        self.depth = depth
        self.done = 0
        for c in self.copies[:depth]:
            c.start()

    def wait(self, part, j):
        while self.done <= self.place[part, j]:
            self.copies[self.done].wait()
            if self.done + self.depth < len(self.copies):
                self.copies[self.done + self.depth].start()
            self.done += 1


def split_qkv(acc):
    w1 = HPB * HD
    zero = jnp.zeros((acc.shape[0], HD), BF)
    q = jnp.concatenate([(acc[:, 0:w1].astype(BF) * 0.125).astype(BF), zero], axis=1)
    k = jnp.concatenate([acc[:, w1 : 2 * w1].astype(BF), zero], axis=1)
    v = jnp.concatenate([acc[:, 2 * w1 : 3 * w1].astype(BF), zero], axis=1)
    return q, k, v


def head_cols(shape, i):
    c = lax.broadcasted_iota(jnp.int32, shape, len(shape) - 1)
    return (c >= i * HD) & (c < (i + 1) * HD)


def spread(x):
    return jnp.concatenate(
        [jnp.where(head_cols(x.shape, i), x, jnp.zeros_like(x)) for i in range(HPB)], axis=0
    )


def gather_heads(x):
    n = x.shape[0] // HPB
    out = jnp.zeros((n, x.shape[1]), x.dtype)
    for i in range(HPB):
        out = jnp.where(head_cols(out.shape, i), x[i * n : (i + 1) * n], out)
    return out


def out_cols(a):
    return jnp.concatenate([jnp.zeros((a.shape[0], HD), a.dtype), a[:, 0 : HPB * HD]], axis=1)


def qkv_kernel(me_ref, tok_ref, w_ref, qkvb_ref, q_ref, k_ref, v_ref, wc, sem):
    nb, d, _ = w_ref.shape
    me = me_ref[0]
    w = Weights(me, w_ref, wc, sem, [(0, j) for j in range(nb)])
    for j in range(nb):
        w.wait(0, j)
        acc = nn(tok_ref[...], wc[j, :, 0 : 3 * HPB * HD]) + qkvb_ref[j ^ me]
        q, k, v = split_qkv(acc)
        q_ref[j] = q
        k_ref[j] = k
        v_ref[j] = v


def qkv_call(me, tok, w, qkvb):
    nb, d, _ = w.shape
    s = tok.shape[0]
    return pl.pallas_call(
        qkv_kernel,
        out_shape=[jax.ShapeDtypeStruct((nb, s, 4 * HD), BF)] * 3,
        in_specs=[sm_spec(), vm_spec(), any_spec(), vm_spec()],
        out_specs=[vm_spec()] * 3,
        scratch_shapes=[pltpu.VMEM((nb, d, d), BF), pltpu.SemaphoreType.DMA((nb,))],
        compiler_params=params(),
        cost_estimate=pl.CostEstimate(
            flops=2 * s * d * 3 * d, bytes_accessed=8 * d * d, transcendentals=0
        ),
        name="qkv",
    )(me, tok, w, qkvb)


def mem_forward_kernel(
    nmem, save, me_ref, m_ref, k_hbm, v_hbm, w_ref, qkvb_ref, ub_ref, vec_ref, *rest
):
    if save:
        (
            z2_ref, qm_ref, km_ref, vm_ref, pm_ref, am_ref, z1b_ref, g_ref, gp_ref, xh1_ref,
            xh2_ref, inv_ref,
        ) = rest[:12]
        rest = rest[12:]
    else:
        z2_ref = rest[0]
        rest = rest[1:]
    wv, kk, vv, sc, sem, sem2 = rest
    nb, d, _ = w_ref.shape
    seg = k_hbm.shape[1]
    mp = m_ref.shape[0]
    keys = seg + mp
    w1 = HPB * HD
    me = me_ref[0]
    w = Weights(
        me, w_ref, wv, sem,
        [(0, j) for j in range(nb)] + [(p, j) for j in range(nb) for p in (1, 2)],
    )
    kc = pltpu.make_async_copy(k_hbm, kk.at[:, 0:seg, :], sem2.at[0])
    vc = pltpu.make_async_copy(v_hbm, vv.at[:, 0:seg, :], sem2.at[1])
    kc.start()
    vc.start()
    mem = m_ref[...]
    mb = mem.astype(BF)
    qs = []
    for j in range(nb):
        w.wait(0, j)
        acc = nn(mb, wv[j, :, 0 : 3 * w1]) + qkvb_ref[j ^ me]
        q, k, v = split_qkv(acc)
        qs.append(q)
        kk[j, seg:keys, :] = k
        vv[j, seg:keys, :] = v
        if save:
            qm_ref[j] = q
            km_ref[j] = k
            vm_ref[j] = v
    kc.wait()
    vc.wait()
    n = HPB * mp
    for j in range(nb):
        sc[j * n : (j + 1) * n, :] = nt(spread(qs[j]), kk[j])
    keep = lax.broadcasted_iota(jnp.int32, (n, keys), 1) < seg + nmem
    heads = []
    for j in range(nb):
        s = jnp.where(keep, sc[j * n : (j + 1) * n, :], NEG)
        e = jnp.exp(s - jnp.max(s, axis=-1, keepdims=True))
        p = (e / jnp.sum(e, axis=-1, keepdims=True)).astype(BF)
        if save:
            pm_ref[j] = p
        heads.append(p)
    out = jnp.zeros((mp, d), F32)
    for j in range(nb):
        a = gather_heads(nn(heads[j], vv[j])).astype(BF)
        if save:
            am_ref[j] = a
        out += nt(out_cols(a), wv[j, :, d - 4 * HD : d])
    xh1, inv1 = norm_stats(mem + out + vec_ref[0:1])
    z1 = xh1 * vec_ref[1:2] + vec_ref[2:3]
    z1b = z1.astype(BF)
    y = jnp.zeros((mp, d), F32)
    for j in range(nb):
        w.wait(1, j)
        f = nn(z1b, wv[j, :, d : 2 * d]) + ub_ref[j ^ me]
        g, gp = gelu_both(f)
        g = g.astype(BF)
        if save:
            g_ref[j] = g
            gp_ref[j] = gp
        w.wait(2, j)
        y += nt(g, wv[j, :, 2 * d : 3 * d])
    xh2, inv2 = norm_stats(z1 + y + vec_ref[3:4])
    z2 = xh2 * vec_ref[4:5] + vec_ref[5:6]
    z2_ref[...] = jnp.where(rows_mask((mp, d), nmem), z2, 0.0)
    if save:
        z1b_ref[...] = z1b
        xh1_ref[...] = xh1
        xh2_ref[...] = xh2
        inv_ref[:, 0:128] = jnp.broadcast_to(inv1, (mp, 128))
        inv_ref[:, 128:256] = jnp.broadcast_to(inv2, (mp, 128))


def mem_forward(me, m, k, v, w, qkvb, ub, vec, nmem, save):
    nb, d, _ = w.shape
    seg = k.shape[1]
    mp = m.shape[0]
    keys = seg + mp
    sds = jax.ShapeDtypeStruct
    shapes = [sds((mp, d), F32)]
    if save:
        shapes += [sds((nb, mp, 4 * HD), BF)] * 3
        shapes += [
            sds((nb, HPB * mp, keys), BF),
            sds((nb, mp, 4 * HD), BF),
            sds((mp, d), BF),
            sds((nb, mp, d), BF),
            sds((nb, mp, d), F32),
            sds((mp, d), F32),
            sds((mp, d), F32),
            sds((mp, 256), F32),
        ]
    return pl.pallas_call(
        functools.partial(mem_forward_kernel, nmem, save),
        out_shape=shapes,
        in_specs=[sm_spec(), vm_spec()] + [any_spec()] * 3 + [vm_spec()] * 3,
        out_specs=[vm_spec()] * len(shapes),
        scratch_shapes=[
            pltpu.VMEM((nb, d, 3 * d), BF),
            pltpu.VMEM((nb, keys, 4 * HD), BF),
            pltpu.VMEM((nb, keys, 4 * HD), BF),
            pltpu.VMEM((nb * HPB * mp, keys), F32),
            pltpu.SemaphoreType.DMA((3 * nb,)),
            pltpu.SemaphoreType.DMA((2,)),
        ],
        compiler_params=params(),
        cost_estimate=pl.CostEstimate(
            flops=2 * mp * d * d * 12, bytes_accessed=24 * d * d, transcendentals=0
        ),
        name="mem_forward_save" if save else "mem_forward",
    )(me, m, k, v, w, qkvb, ub, vec)


def colsum(x):
    return jnp.sum(x, axis=0, keepdims=True)


CH = 64


def token_kernel(
    nmem,
    me_ref,
    tok_ref,
    ct_ref,
    live_ref,
    m_ref,
    q_hbm,
    k_hbm,
    v_hbm,
    w_ref,
    qkvb_ref,
    ub_ref,
    vec_ref,
    out_ref,
    z1b_ref,
    a_ref,
    g_ref,
    gf_ref,
    gr2b_ref,
    gr1_ref,
    gq_ref,
    gk_ref,
    gv_ref,
    base_ref,
    small_ref,
    ubg_ref,
    wv,
    qq,
    kk,
    vv,
    probs,
    big,
    one,
    xh1,
    g1b,
    inv,
    gp,
    sem,
    sem2,
):
    nb, d, _ = w_ref.shape
    seg = tok_ref.shape[0]
    mp = m_ref.shape[0]
    keys = seg + mp
    w1 = HPB * HD
    steps = seg // CH
    me = me_ref[0]
    w = Weights(me, w_ref, wv, sem, [(p, j) for p in range(3) for j in range(nb)])
    loads = [
        pltpu.make_async_copy(q_hbm, qq, sem2.at[0]),
        pltpu.make_async_copy(k_hbm, kk.at[:, 0:seg, :], sem2.at[1]),
        pltpu.make_async_copy(v_hbm, vv.at[:, 0:seg, :], sem2.at[2]),
    ]
    for c in loads:
        c.start()
    mb = m_ref[...].astype(BF)
    for j in range(nb):
        w.wait(0, j)
        _, k, v = split_qkv(nn(mb, wv[j, :, 0 : 3 * w1]) + qkvb_ref[j ^ me])
        kk[j, seg:keys, :] = k
        vv[j, seg:keys, :] = v
    for c in loads:
        c.wait()
    one[...] = jnp.zeros_like(one)
    tail = seg + (nmem // 8) * 8

    def attend(j, _):
        vt = vv[j].astype(F32).T.astype(BF)
        parts = []
        for i in range(HPB):
            cols = slice(i * HD, (i + 1) * HD)
            big[0:keys, 0:seg] = nt(kk[j, :, cols], qq[j, :, cols])
            big[tail:keys, 0:seg] = jnp.where(
                rows_mask((keys - tail, seg), seg + nmem - tail), big[tail:keys, 0:seg], NEG
            )
            for c in range(seg // 128):
                cols = slice(c * 128, (c + 1) * 128)
                s = big[0:keys, cols]
                e = jnp.exp(s - jnp.max(s, axis=0, keepdims=True))
                p = e * (1.0 / jnp.sum(e, axis=0, keepdims=True))
                probs[j * HPB + i, :, cols] = p.astype(BF)
            parts.append(nn(vt[i * HD : (i + 1) * HD], probs[j * HPB + i]))
        parts.append(jnp.zeros((HD, seg), F32))
        a = jnp.concatenate(parts, axis=0).T.astype(BF)
        a_ref[j] = a
        one[...] += nt(out_cols(a), wv[j, :, d - 4 * HD : d])
        return 0

    lax.fori_loop(0, nb, attend, 0)

    def first(c, _):
        rows = pl.ds(pl.multiple_of(c * CH, CH), CH)
        r = tok_ref[rows, :].astype(F32) + one[rows, :] + vec_ref[0:1]
        x, v = norm_stats(r)
        xh1[rows, :] = x
        inv[rows, 0:128] = jnp.broadcast_to(v, (CH, 128))
        z1 = x * vec_ref[1:2] + vec_ref[2:3]
        z1b_ref[rows, :] = z1.astype(BF)
        one[rows, :] = z1 + vec_ref[3:4]
        return 0

    lax.fori_loop(0, steps, first, 0)
    w.wait(2, nb - 1)

    def feed(j, _):
        big[0:seg, 0:d] = nn(z1b_ref[...], wv[j, :, d : 2 * d])

        def act(c, _):
            rows = pl.ds(pl.multiple_of(c * 32, 32), 32)
            g, p = gelu_both(big[rows, 0:d] + ub_ref[j ^ me])
            g_ref[j, rows, :] = g.astype(BF)
            gp[j, rows, :] = p.astype(BF)
            return 0

        lax.fori_loop(0, seg // 32, act, 0)
        one[...] += nt(g_ref[j], wv[j, :, 2 * d : 3 * d])
        return 0

    lax.fori_loop(0, nb, feed, 0)
    zero = jnp.zeros((1, d), F32)

    def second(c, carry):
        sg, ss, sb = carry
        rows = pl.ds(pl.multiple_of(c * CH, CH), CH)
        x, v = norm_stats(one[rows, :])
        out_ref[rows, :] = ((x * vec_ref[4:5] + vec_ref[5:6]) * live_ref[0:1, 0:1]).astype(BF)
        gz = ct_ref[rows, :].astype(F32) * live_ref[0:1, 0:1]
        gr = norm_back(gz * vec_ref[4:5], x, v)
        one[rows, :] = gr
        gr2b_ref[rows, :] = gr.astype(BF)
        return (sg + colsum(gz * x), ss + colsum(gz), sb + colsum(gr))

    sg, ss, sb = lax.fori_loop(0, steps, second, (zero, zero, zero))
    small_ref[3:4] = sb
    small_ref[4:5] = sg
    small_ref[5:6] = ss

    def feed_back(j, _):
        big[0:seg, 0:d] = nn(gr2b_ref[...], wv[j, :, 2 * d : 3 * d])

        def act(c, total):
            rows = pl.ds(pl.multiple_of(c * CH, CH), CH)
            gf = (big[rows, 0:d] * gp[j, rows, :].astype(F32)).astype(BF)
            gf_ref[j, rows, :] = gf
            return total + colsum(gf.astype(F32))

        ubg_ref[j] = lax.fori_loop(0, steps, act, zero)
        one[...] += nt(gf_ref[j], wv[j, :, d : 2 * d])
        return 0

    lax.fori_loop(0, nb, feed_back, 0)

    def first_back(c, carry):
        sg, ss, sb = carry
        rows = pl.ds(pl.multiple_of(c * CH, CH), CH)
        gz = one[rows, :]
        x = xh1[rows, :]
        gr = norm_back(gz * vec_ref[1:2], x, inv[rows, 0:1])
        gr1_ref[rows, :] = gr
        g1b[rows, :] = gr.astype(BF)
        return (sg + colsum(gz * x), ss + colsum(gz), sb + colsum(gr))

    sg, ss, sb = lax.fori_loop(0, steps, first_back, (zero, zero, zero))
    small_ref[0:1] = sb
    small_ref[1:2] = sg
    small_ref[2:3] = ss
    small_ref[6:8] = jnp.zeros((2, d), F32)

    def attend_back(j, base):
        ga = nn(g1b[...], wv[j, :, d - 4 * HD : d])[:, HD:]
        gab = ga.astype(BF)
        delta = (gab.astype(F32) * a_ref[j, :, 0:w1].astype(F32)).T
        kt = kk[j].astype(F32).T.astype(BF)
        gqs = []
        gks = []
        gvs = []
        for i in range(HPB):
            cols = slice(i * HD, (i + 1) * HD)
            g = gab[:, cols]
            p = probs[j * HPB + i]
            dl = jnp.sum(delta[cols], axis=0, keepdims=True)
            gvs.append(nn(p, g))
            gs = (p.astype(F32) * (nt(vv[j, :, cols], g) - dl)).astype(BF)
            gks.append(nn(gs, qq[j, :, cols]))
            gqs.append(nn(kt[cols], gs))
        zq = jnp.zeros((HD, seg), F32)
        zk = jnp.zeros((keys, HD), F32)
        gq_ref[j] = (jnp.concatenate(gqs + [zq], axis=0).T * 0.125).astype(BF)
        gk = jnp.concatenate(gks + [zk], axis=1)
        gv = jnp.concatenate(gvs + [zk], axis=1)
        gk_ref[j] = gk
        gv_ref[j] = gv
        gm = jnp.concatenate(
            [jnp.zeros((mp, w1), F32), gk[seg:keys, 0:w1], gv[seg:keys, 0:w1]], axis=1
        ).astype(BF)
        return base + nt(gm, wv[j, :, 0 : 3 * w1])

    base_ref[...] = lax.fori_loop(0, nb, attend_back, jnp.zeros((mp, d), F32))


def token_call(me, tok, ct, live, m, q, k, v, w, qkvb, ub, vec, nmem):
    nb, d, _ = w.shape
    seg = tok.shape[0]
    mp = m.shape[0]
    keys = seg + mp
    sds = jax.ShapeDtypeStruct
    shapes = [
        sds((seg, d), BF),
        sds((seg, d), BF),
        sds((nb, seg, 4 * HD), BF),
        sds((nb, seg, d), BF),
        sds((nb, seg, d), BF),
        sds((seg, d), BF),
        sds((seg, d), F32),
        sds((nb, seg, 4 * HD), BF),
        sds((nb, keys, 4 * HD), F32),
        sds((nb, keys, 4 * HD), F32),
        sds((mp, d), F32),
        sds((8, d), F32),
        sds((nb, 1, d), F32),
    ]
    return pl.pallas_call(
        functools.partial(token_kernel, nmem),
        out_shape=shapes,
        in_specs=[sm_spec()] + [vm_spec()] * 4 + [any_spec()] * 4 + [vm_spec()] * 3,
        out_specs=[vm_spec()] * len(shapes),
        scratch_shapes=[
            pltpu.VMEM((nb, d, 3 * d), BF),
            pltpu.VMEM((nb, seg, 4 * HD), BF),
            pltpu.VMEM((nb, keys, 4 * HD), BF),
            pltpu.VMEM((nb, keys, 4 * HD), BF),
            pltpu.VMEM((nb * HPB, keys, seg), BF),
            pltpu.VMEM((keys, d), F32),
            pltpu.VMEM((seg, d), F32),
            pltpu.VMEM((seg, d), F32),
            pltpu.VMEM((seg, d), BF),
            pltpu.VMEM((seg, 128), F32),
            pltpu.VMEM((nb, seg, d), BF),
            pltpu.SemaphoreType.DMA((3 * nb,)),
            pltpu.SemaphoreType.DMA((3,)),
        ],
        compiler_params=params(),
        cost_estimate=pl.CostEstimate(
            flops=5 * seg * d * d * 12, bytes_accessed=60 * d * d, transcendentals=0
        ),
        name="token_rows",
    )(me, tok, ct, live, m, q, k, v, w, qkvb, ub, vec)


def back_feed(w, wv, nb, d, gz, vec_ref, gp_ref, xh1, xh2, inv_ref, gf_ref=None, ubg_ref=None):
    gr2 = norm_back(gz * vec_ref[4:5], xh2, inv_ref[:, 128:129])
    gr2b = gr2.astype(BF)
    acc = gr2
    for j in range(nb):
        w.wait(2, j)
        gf = (nn(gr2b, wv[j, :, 2 * d : 3 * d]) * gp_ref[j]).astype(BF)
        if gf_ref is not None:
            gf_ref[j] = gf
            ubg_ref[j] = colsum(gf.astype(F32))
        w.wait(1, j)
        acc += nt(gf, wv[j, :, d : 2 * d])
    return gr2, acc, norm_back(acc * vec_ref[1:2], xh1, inv_ref[:, 0:1])


def back_scores(j, gab, am_ref, pm_ref, vv, delta_rows):
    n = HPB * delta_rows
    gs3 = spread(gab)
    a3 = jnp.concatenate([am_ref[j]] * HPB, axis=0)
    dl = jnp.sum(gs3.astype(F32) * a3.astype(F32), axis=1, keepdims=True)
    p = pm_ref[j].astype(F32)
    return gs3, p, (p * (nt(gs3, vv[j]) - dl)).astype(BF)


def mem_backward_kernel(
    nmem, me_ref, g_ref, k_hbm, v_hbm, w_ref, vec_ref, base_ref, qm_ref, km_ref, vm_ref, pm_ref,
    am_ref, gp_ref, xh1_ref, xh2_ref, inv_ref, gm_ref, wv, kk, vv, sem, sem2
):
    nb, d, _ = w_ref.shape
    seg = k_hbm.shape[1]
    mp = g_ref.shape[0]
    keys = seg + mp
    w1 = HPB * HD
    w = Weights(
        me_ref[0], w_ref, wv, sem,
        [(p, j) for j in range(nb) for p in (2, 1)] + [(0, j) for j in range(nb)],
    )
    kc = pltpu.make_async_copy(k_hbm, kk.at[:, 0:seg, :], sem2.at[0])
    vc = pltpu.make_async_copy(v_hbm, vv.at[:, 0:seg, :], sem2.at[1])
    kc.start()
    vc.start()
    kk[:, seg:keys, :] = km_ref[...]
    vv[:, seg:keys, :] = vm_ref[...]
    _, _, gr1 = back_feed(
        w, wv, nb, d, g_ref[...], vec_ref, gp_ref, xh1_ref[...], xh2_ref[...], inv_ref
    )
    gr1b = gr1.astype(BF)
    kc.wait()
    vc.wait()
    gabs = []
    for j in range(nb):
        w.wait(0, j)
        ga = nn(gr1b, wv[j, :, d - 4 * HD : d]).astype(BF)
        gabs.append(jnp.concatenate([ga[:, HD:], jnp.zeros((mp, HD), BF)], axis=1))
    scores = [back_scores(j, gabs[j], am_ref, pm_ref, vv, mp) for j in range(nb)]
    out = gr1 + base_ref[...]
    for j in range(nb):
        gs3, p, gs = scores[j]
        gq = gather_heads(nn(gs, kk[j])) * 0.125
        gk = nn(gs[:, seg:keys].astype(F32).T.astype(BF), spread(qm_ref[j]))
        gv = nn(p[:, seg:keys].T.astype(BF), gs3)
        gm = jnp.concatenate([gq[:, 0:w1], gk[:, 0:w1], gv[:, 0:w1]], axis=1).astype(BF)
        out += nt(gm, wv[j, :, 0 : 3 * w1])
    gm_ref[...] = out


def mem_backward(me, g, k, v, w, vec, base, saved):
    nb, d, _ = w.shape
    seg = k.shape[1]
    mp = g.shape[0]
    keys = seg + mp
    qm, km, vm, pm, am, _, _, gp, xh1, xh2, inv = saved
    args = (me, g, k, v, w, vec, base, qm, km, vm, pm, am, gp, xh1, xh2, inv)
    return pl.pallas_call(
        functools.partial(mem_backward_kernel, 0),
        out_shape=jax.ShapeDtypeStruct((mp, d), F32),
        in_specs=[sm_spec(), vm_spec()] + [any_spec()] * 3 + [vm_spec()] * 11,
        out_specs=vm_spec(),
        scratch_shapes=[
            pltpu.VMEM((nb, d, 3 * d), BF),
            pltpu.VMEM((nb, keys, 4 * HD), BF),
            pltpu.VMEM((nb, keys, 4 * HD), BF),
            pltpu.SemaphoreType.DMA((3 * nb,)),
            pltpu.SemaphoreType.DMA((2,)),
        ],
        compiler_params=params(),
        cost_estimate=pl.CostEstimate(
            flops=2 * mp * d * d * 12, bytes_accessed=24 * d * d, transcendentals=0
        ),
        name="mem_backward",
    )(*args)


def last_feed_kernel(
    me_ref, g_ref, w_ref, vec_ref, gp_ref, xh1_ref, xh2_ref, inv_ref, gr2b_ref, gf_ref, gr1_ref,
    small_ref, ubg_ref, wv, sem
):
    nb, d, _ = w_ref.shape
    w = Weights(me_ref[0], w_ref, wv, sem, [(p, j) for j in range(nb) for p in (2, 1)])
    gz = g_ref[...]
    xh1 = xh1_ref[...]
    xh2 = xh2_ref[...]
    gr2, gz1, gr1 = back_feed(
        w, wv, nb, d, gz, vec_ref, gp_ref, xh1, xh2, inv_ref, gf_ref, ubg_ref
    )
    gr2b_ref[...] = gr2.astype(BF)
    gr1_ref[...] = gr1
    small_ref[0:1] = colsum(gr1)
    small_ref[1:2] = colsum(gz1 * xh1)
    small_ref[2:3] = colsum(gz1)
    small_ref[3:4] = colsum(gr2)
    small_ref[4:5] = colsum(gz * xh2)
    small_ref[5:6] = colsum(gz)
    small_ref[6:8] = jnp.zeros((2, d), F32)


def last_feed(me, g, w, vec, saved):
    nb, d, _ = w.shape
    mp = g.shape[0]
    _, _, _, _, _, _, _, gp, xh1, xh2, inv = saved
    sds = jax.ShapeDtypeStruct
    shapes = [
        sds((mp, d), BF),
        sds((nb, mp, d), BF),
        sds((mp, d), F32),
        sds((8, d), F32),
        sds((nb, 1, d), F32),
    ]
    return pl.pallas_call(
        last_feed_kernel,
        out_shape=shapes,
        in_specs=[sm_spec(), vm_spec(), any_spec()] + [vm_spec()] * 5,
        out_specs=[vm_spec()] * len(shapes),
        scratch_shapes=[pltpu.VMEM((nb, d, 3 * d), BF), pltpu.SemaphoreType.DMA((2 * nb,))],
        compiler_params=params(),
        cost_estimate=pl.CostEstimate(
            flops=2 * mp * d * d * 8, bytes_accessed=16 * d * d, transcendentals=0
        ),
        name="last_feed",
    )(me, g, w, vec, gp, xh1, xh2, inv)


def last_attention_kernel(
    me_ref, gr1m_ref, k_hbm, v_hbm, w_ref, qm_ref, km_ref, vm_ref, pm_ref, am_ref, gq_ref, gk_ref,
    gv_ref, gr1_ref, gm_ref, gqkv_ref, ig_ref, qvb_ref, wv, kk, vv, one, sem, sem2
):
    nb, d, _ = w_ref.shape
    seg = k_hbm.shape[1]
    mp = gr1m_ref.shape[0]
    keys = seg + mp
    w1 = HPB * HD
    w = Weights(me_ref[0], w_ref, wv, sem, [(0, j) for j in range(nb)])
    kc = pltpu.make_async_copy(k_hbm, kk.at[:, 0:seg, :], sem2.at[0])
    vc = pltpu.make_async_copy(v_hbm, vv.at[:, 0:seg, :], sem2.at[1])
    kc.start()
    vc.start()
    kk[:, seg:keys, :] = km_ref[...]
    vv[:, seg:keys, :] = vm_ref[...]
    gr1 = gr1m_ref[...]
    gr1b = gr1.astype(BF)
    kc.wait()
    vc.wait()
    gabs = []
    for j in range(nb):
        w.wait(0, j)
        ga = nn(gr1b, wv[j, :, d - 4 * HD : d]).astype(BF)
        gabs.append(jnp.concatenate([ga[:, HD:], jnp.zeros((mp, HD), BF)], axis=1))
    scores = [back_scores(j, gabs[j], am_ref, pm_ref, vv, mp) for j in range(nb)]
    out = gr1
    for j in range(nb):
        gs3, p, gs = scores[j]
        gq = (gather_heads(nn(gs, kk[j])) * 0.125).astype(BF)
        gk = (gk_ref[j] + nn(gs.astype(F32).T.astype(BF), spread(qm_ref[j]))).astype(BF)
        gv = (gv_ref[j] + nn(p.T.astype(BF), gs3)).astype(BF)
        gqt = gq_ref[j]
        gqkv_ref[j, 0:seg, 0:w1] = gqt[:, 0:w1]
        gqkv_ref[j, seg:keys, 0:w1] = gq[:, 0:w1]
        gqkv_ref[j, :, w1 : 2 * w1] = gk[:, 0:w1]
        gqkv_ref[j, :, 2 * w1 : 3 * w1] = gv[:, 0:w1]
        qvb_ref[j, 0:1, :] = colsum(gqt.astype(F32)) + colsum(gq.astype(F32))
        qvb_ref[j, 1:2, :] = colsum(gv.astype(F32))
        x = nt(gqkv_ref[j, 0:seg, :], wv[j, :, 0 : 3 * w1])
        if j == 0:
            one[...] = gr1_ref[...] + x
        else:
            one[...] += x
        out += nt(gqkv_ref[j, seg:keys, :], wv[j, :, 0 : 3 * w1])
    gm_ref[...] = out
    ig_ref[...] = one[...].astype(BF)


def last_attention(me, gr1m, k, v, w, saved, gq, gk, gv, gr1):
    nb, d, _ = w.shape
    seg = k.shape[1]
    mp = gr1m.shape[0]
    keys = seg + mp
    w1 = HPB * HD
    qm, km, vm, pm, am, _, _, _, _, _, _ = saved
    sds = jax.ShapeDtypeStruct
    shapes = [
        sds((mp, d), F32),
        sds((nb, keys, 3 * w1), BF),
        sds((seg, d), BF),
        sds((nb, 2, 4 * HD), F32),
    ]
    return pl.pallas_call(
        last_attention_kernel,
        out_shape=shapes,
        in_specs=[sm_spec(), vm_spec()] + [any_spec()] * 3 + [vm_spec()] * 9,
        out_specs=[vm_spec()] * len(shapes),
        scratch_shapes=[
            pltpu.VMEM((nb, d, d), BF),
            pltpu.VMEM((nb, keys, 4 * HD), BF),
            pltpu.VMEM((nb, keys, 4 * HD), BF),
            pltpu.VMEM((seg, d), F32),
            pltpu.SemaphoreType.DMA((nb,)),
            pltpu.SemaphoreType.DMA((2,)),
        ],
        compiler_params=params(),
        cost_estimate=pl.CostEstimate(
            flops=2 * seg * d * d * 4, bytes_accessed=30 * d * d, transcendentals=0
        ),
        name="last_attention",
    )(me, gr1m, k, v, w, qm, km, vm, pm, am, gq, gk, gv, gr1)


def turn(dst, t, a_ref, b_ref):
    seg = a_ref.shape[0]
    dst[t, :, 0:seg] = a_ref[...].astype(F32).T.astype(BF)
    dst[t, :, seg:] = b_ref[...].astype(F32).T.astype(BF)


def feed_grad_kernel(l_ref, lm_ref, r_ref, rm_ref, keep_ref, send_ref, lt):
    seg = l_ref.shape[0]

    @pl.when(pl.program_id(0) == 0)
    def _():
        turn(lt, 0, l_ref, lm_ref)

    for c, o in enumerate((keep_ref, send_ref)):
        o[0] = (nn(lt[0, :, 0:seg], r_ref[c]) + nn(lt[0, :, seg:], rm_ref[c])).astype(BF)


def feed_grad(left, left_m, right, right_m):
    seg, d = left.shape
    mp = left_m.shape[0]
    nb, _, cols = right.shape
    whole = lambda y: (0, 0)
    block = lambda y: (y, 0, 0)
    return pl.pallas_call(
        feed_grad_kernel,
        grid=(nb // 2,),
        out_shape=[jax.ShapeDtypeStruct((nb // 2, d, cols), BF)] * 2,
        in_specs=[
            pl.BlockSpec((seg, d), whole),
            pl.BlockSpec((mp, d), whole),
            pl.BlockSpec((2, seg, cols), block),
            pl.BlockSpec((2, mp, cols), block),
        ],
        out_specs=[pl.BlockSpec((1, d, cols), block)] * 2,
        scratch_shapes=[pltpu.VMEM((1, d, seg + mp), BF)],
        compiler_params=params(),
        cost_estimate=pl.CostEstimate(
            flops=2 * seg * d * cols * nb, bytes_accessed=16 * d * d, transcendentals=0
        ),
        name="feed_grad",
    )(left, left_m, right, right_m)


def attention_grad_kernel(
    tok_ref, m_ref, gqkv_ref, gr1_ref, gr1m_ref, a_ref, am_ref, small_ref, keep_ref, send_ref, lt
):
    seg, d = tok_ref.shape
    w1 = HPB * HD
    _, nd, n, _ = keep_ref.shape
    chunk = d // nd

    @pl.when(pl.program_id(0) == 0)
    def _():
        turn(lt, 0, tok_ref, m_ref)
        turn(lt, 1, gr1_ref, gr1m_ref)

    for c, o in enumerate((keep_ref, send_ref)):
        x = nn(lt[0], gqkv_ref[c])
        y = nn(lt[1, :, 0:seg], a_ref[c]) + nn(lt[1, :, seg:], am_ref[c])
        x = jnp.concatenate([x, y[:, 0:w1]], axis=1).astype(BF)
        for i in range(nd):
            o[0, i, 0:chunk, :] = x[i * chunk : (i + 1) * chunk]
            if n > chunk:
                o[0, i, chunk:n, :] = small_ref[c, i]


def attention_grad(tok, m, gqkv, gr1, gr1m, a, am, small):
    seg, d = tok.shape
    mp = m.shape[0]
    nb, keys, w3 = gqkv.shape
    _, nd, extra, _ = small.shape
    n = d // nd + extra
    whole = lambda y: (0, 0)
    block = lambda y: (y, 0, 0)
    block4 = lambda y: (y, 0, 0, 0)
    return pl.pallas_call(
        attention_grad_kernel,
        grid=(nb // 2,),
        out_shape=[jax.ShapeDtypeStruct((nb // 2, nd, n, d), BF)] * 2,
        in_specs=[
            pl.BlockSpec((seg, d), whole),
            pl.BlockSpec((mp, d), whole),
            pl.BlockSpec((2, keys, w3), block),
            pl.BlockSpec((seg, d), whole),
            pl.BlockSpec((mp, d), whole),
            pl.BlockSpec((2, seg, 4 * HD), block),
            pl.BlockSpec((2, mp, 4 * HD), block),
            pl.BlockSpec((2, nd, extra, d), block4),
        ],
        out_specs=[pl.BlockSpec((1, nd, n, d), block4)] * 2,
        scratch_shapes=[pltpu.VMEM((2, d, keys), BF)],
        compiler_params=params(),
        cost_estimate=pl.CostEstimate(
            flops=2 * seg * d * d * 4, bytes_accessed=16 * d * d, transcendentals=0
        ),
        name="attention_grad",
    )(tok, m, gqkv, gr1, gr1m, a, am, small)


def pack_kernel(q_ref, k_ref, v_ref, o_ref, u_ref, d_ref, out_ref):
    n, w1 = q_ref.shape
    d = u_ref.shape[1]
    for i, r in enumerate((q_ref, k_ref, v_ref)):
        out_ref[:, i * w1 : (i + 1) * w1] = r[...]
    out_ref[:, 3 * w1 : 4 * w1] = o_ref[...].astype(F32).T.astype(BF)
    out_ref[:, d : 2 * d] = u_ref[...]
    out_ref[:, 2 * d : 3 * d] = d_ref[...].astype(F32).T.astype(BF)


def pack(*weights):
    n = weights[0].shape[0]
    d = weights[4].shape[1]
    return pl.pallas_call(
        pack_kernel,
        out_shape=jax.ShapeDtypeStruct((n, 3 * d), BF),
        in_specs=[vm_spec()] * 6,
        out_specs=vm_spec(),
        name="pack",
    )(*weights)


def flip(a, axis, bit):
    return lax.ppermute(a, axis, [(i, i ^ bit) for i in range(lax.axis_size(axis))])


def shift(a, by):
    n = lax.axis_size("dp")
    return lax.ppermute(a, "dp", [(i, (i + by) % n) for i in range(n)])


def add(*xs):
    total = xs[0].astype(F32)
    for x in xs[1:]:
        total = total + x.astype(F32)
    return total.astype(BF)


def pick(a, i, axis):
    return lax.dynamic_index_in_dim(a, i, axis, keepdims=False)


def y_half(a):
    return add(a[0], flip(a[1], "mp", 2))


def x_half(a, axis):
    b = lax.axis_index("dp") % 2
    return add(pick(a, b, axis), flip(pick(a, 1 - b, axis), "dp", 1))


def z_quarter(a):
    z = lax.axis_index("dp") // 2
    part = [pick(a, (z + i) % 4, 0) for i in range(4)]
    return add(part[0], shift(part[1], 2), shift(part[3], -2), shift(part[2], 4))


def reduce_blocks(keep, send):
    _, _, n, c = keep.shape
    t = add(keep, flip(send, "mp", 1)).reshape(2, 4, 2, n, c)
    half = c // 2
    first = y_half(x_half(t[..., :half], 2))
    second = x_half(y_half(t[..., half:]), 1)
    s = z_quarter(jnp.stack([first, second], 1))
    return jnp.concatenate([s[0], s[1]], axis=1)


def relative(x):
    me = lax.axis_index("mp")
    v = x.reshape((2, 2) + x.shape[1:])
    v = jnp.where(me % 2 == 1, v[:, ::-1], v)
    v = jnp.where(me // 2 == 1, v[::-1], v)
    return v.reshape(x.shape)


def gather_small(x):
    nd = lax.axis_size("dp")
    nb = lax.axis_size("mp")
    if nd != 8:
        return lax.all_gather(x, ("mp", "dp"), axis=0).reshape(nb, nd, -1)
    k = x.shape[0]
    t = x.reshape(1, k)
    me = lax.axis_index("dp")
    b = me % 2
    z = me // 2
    o = flip(t, "mp", 1)
    c = lax.axis_index("mp") % 2
    t = jnp.where(c == 0, jnp.concatenate([t, o]), jnp.concatenate([o, t]))
    o = flip(t, "mp", 2)
    y = lax.axis_index("mp") // 2
    t = jnp.where(y == 0, jnp.concatenate([t, o]), jnp.concatenate([o, t]))
    o = flip(t, "dp", 1)
    t = jnp.where(b == 0, jnp.stack([t, o]), jnp.stack([o, t]))
    up, down, far = shift(t, -2), shift(t, 2), shift(t, 4)
    ring = jnp.stack([t, up, far, down, t, up, far])
    t = lax.dynamic_slice_in_dim(ring, (4 - z) % 4, 4, 0)
    return t.reshape(nd, nb, k).transpose(1, 0, 2)


def body(
    tokens, memory_init, query_weight, query_bias, key_weight, value_weight, value_bias, out_weight,
    out_bias, first_gain, first_shift, up_weight, up_bias, down_weight, down_bias, second_gain,
    second_shift, cotangent, group_segs, chain_group
):
    nd = lax.axis_size("dp")
    nb = lax.axis_size("mp")
    me = lax.axis_index("mp")
    me1 = me.astype(jnp.int32).reshape(1)
    segments = tokens.shape[1]
    d = tokens.shape[3]
    part = tokens.shape[2]
    seg = part * nb
    nmem = memory_init.shape[0] * nb
    pad = -(-nmem // 16) * 16
    both = ("mp", "dp")
    wl = pack(query_weight, key_weight, value_weight, out_weight, up_weight, down_weight)
    w = lax.all_gather(wl, both, axis=0).reshape(nb, d, 3 * d)
    vecs = (out_bias, first_gain, first_shift, down_bias, second_gain, second_shift)
    small = jnp.concatenate(
        (query_bias, value_bias, up_bias) + vecs + (memory_init.reshape(-1),)
    )
    n1 = query_bias.shape[0]
    n2 = up_bias.shape[0]
    sg = gather_small(small)
    qb = sg[:, :, 0:n1].reshape(nb, 1, -1).astype(F32)
    vb = sg[:, :, n1 : 2 * n1].reshape(nb, 1, -1).astype(F32)
    qkvb = jnp.concatenate([qb, jnp.zeros_like(qb), vb], axis=2)
    ub = sg[:, :, 2 * n1 : 2 * n1 + n2].reshape(nb, 1, -1).astype(F32)
    at = 2 * n1 + n2
    vec = sg[:, :, at : at + 6 * n1].reshape(nb, nd, 6, n1).transpose(2, 1, 0, 3).reshape(6, d)
    vec = jnp.pad(vec.astype(F32), ((0, 2), (0, 0)))
    ml = memory_init.shape[0]
    m0 = sg[:, :, at + 6 * n1 :].reshape(nb, nd, ml, -1).transpose(0, 2, 1, 3).reshape(nmem, d)
    m0 = jnp.pad(m0.astype(F32), ((0, pad - nmem), (0, 0)))
    tok = lax.all_to_all(tokens[0], "mp", 0, 1, tiled=True).reshape(seg, d)
    ct = lax.all_to_all(cotangent[0], "mp", 0, 1, tiled=True).reshape(seg, d)
    match = chain_group[:, None] == jnp.arange(group_segs.shape[0], dtype=jnp.int32)[None, :]
    count = jnp.sum(jnp.where(match, group_segs[None, :], 0))
    live = (me < count).astype(F32)
    live2 = jnp.full((8, 128), live, F32)
    q, k, v = qkv_call(me1, tok, w, qkvb)
    m = jnp.where(me == 0, m0, 0.0)
    own = m
    for s in range(segments - 1):
        (z,) = mem_forward(me1, m, k, v, w, qkvb, ub, vec, nmem, False)
        m = lax.ppermute(z, "mp", [(s, s + 1)])
        own = own + m
    (out, z1b, a, g, gf, gr2b, gr1, gq, gk, gv, base, sm, ubg) = token_call(
        me1, tok, ct, live2, own, q, k, v, w, qkvb, ub, vec, nmem
    )
    z2m, *saved = mem_forward(me1, own, k, v, w, qkvb, ub, vec, nmem, True)
    am, z1m, g_m = saved[4:7]
    send = base
    gin = jnp.zeros_like(base)
    for s in reversed(range(segments - 1)):
        recv = lax.ppermute(send, "mp", [(s + 1, s)])
        gin = gin + recv
        if s > 0:
            send = mem_backward(me1, recv, k, v, w, vec, base, saved)
    gr2m, gfm, gr1m, smm, ubgm = last_feed(me1, gin, w, vec, saved)
    up_g = feed_grad(z1b, z1m, gf, gfm)
    down_g = feed_grad(gr2b, gr2m, g, g_m)
    gm, gqkv, ig, qvb = last_attention(me1, gr1m, k, v, w, saved, gq, gk, gv, gr1)
    chains = nd * tokens.shape[0]
    norm = live * jnp.sum(z2m * z2m) / (nmem * d * chains)
    norms = jnp.where(jnp.arange(segments) == me, norm, 0.0)
    w1 = d // nb
    smt = (sm + smm)[0:6].reshape(6, nd, nb, n1).transpose(2, 1, 0, 3).reshape(nb, nd, 6 * n1)
    gmi = jnp.where(me == 0, gm[0:nmem], 0.0).reshape(nb, ml, nd, d // nd).transpose(0, 2, 1, 3)
    moved = relative(jnp.concatenate([smt, gmi.reshape(nb, nd, -1)], axis=2))
    qbg = qvb[:, 0, 0:w1].reshape(nb, nd, n1)
    vbg = qvb[:, 1, 0:w1].reshape(nb, nd, n1)
    ubt = (ubg + ubgm).reshape(nb, nd, n2)
    smalls = jnp.concatenate([qbg, vbg, ubt, moved], axis=2)
    count_small = smalls.shape[2]
    tuned = nd == 8
    if tuned:
        rows = jnp.stack(
            [smalls, jnp.zeros_like(smalls).at[:, :, 0:segments].set(norms)], axis=2
        )
        rows = jnp.pad(rows, ((0, 0), (0, 0), (0, 6), (0, 0))).astype(BF)
    else:
        rows = jnp.zeros((nb, 8, 8, d), BF)
    att_g = attention_grad(tok, own, gqkv, gr1, gr1m, a, am, rows)
    chunk = d // nd
    if tuned:
        wup = reduce_blocks(*[x.reshape(2, nd, chunk, d) for x in up_g]).astype(F32)
        wdn = reduce_blocks(*[x.reshape(2, nd, chunk, d) for x in down_g]).astype(F32)
        watt = reduce_blocks(*att_g).astype(F32)
        sr = watt[chunk]
        norms = watt[chunk + 1, 0:segments]
        watt = watt[0:chunk]
    else:

        def scatter(keep, send):
            x = relative(jnp.stack([keep, send], axis=1).reshape(nb, d, d))
            x = x.reshape(nb * nd, chunk, d)
            return lax.psum_scatter(x, both, scatter_dimension=0, tiled=False).astype(F32)

        att_g = [x[:, :, 0 : d // 8] for x in att_g]
        wup, wdn, watt = scatter(*up_g), scatter(*down_g), scatter(*att_g)
        sr = jnp.concatenate(
            [relative(smalls), jnp.broadcast_to(norms, (nb, nd, segments))], axis=2
        ).reshape(nb * nd, -1)
        sr = lax.psum_scatter(sr, both, scatter_dimension=0, tiled=False)
        norms = sr[count_small:]
    vg = sr[at : at + 6 * n1].reshape(6, n1)
    layer_out = lax.all_to_all(out.reshape(nb, part, d), "mp", 0, 0, tiled=True)
    input_grad = lax.all_to_all(ig.reshape(nb, part, d), "mp", 0, 0, tiled=True)
    return (
        layer_out[None],
        input_grad[None],
        sr[at + 6 * n1 : count_small].reshape(ml, d // nd),
        watt[:, 0:w1],
        sr[0:n1],
        watt[:, w1 : 2 * w1],
        watt[:, 2 * w1 : 3 * w1],
        sr[n1 : 2 * n1],
        watt[:, 3 * w1 : d].T,
        vg[0],
        vg[1],
        vg[2],
        wup,
        sr[2 * n1 : at],
        wdn.T,
        vg[3],
        vg[4],
        vg[5],
        norms,
    )


def solution(mesh):
    rows = P("dp", None, "mp", None)
    md, dm = P(("mp", "dp")), P(("dp", "mp"))
    win, wout = P("dp", "mp"), P("mp", "dp")
    in_specs = (
        rows, wout, win, md, win, win, md, wout, dm, dm, dm, win, md, wout, dm, dm, dm, rows, P(),
        P("dp"),
    )
    out_specs = (
        rows, rows, wout, win, md, win, win, md, wout, dm, dm, dm, win, md, wout, dm, dm, dm, P(),
    )
    return jax.shard_map(body, mesh=mesh, in_specs=in_specs, out_specs=out_specs, check_vma=False)
```

time: 652 us -> 481 us (0.74)
  waiting for transfers between devices: 273 us -> 168 us
  blocking collectives: 86 us -> 0 us
  starting transfers between devices: 18.9 us -> 68 us
  Pallas kernels: 208 us -> 178 us
  local copies, waits for them, and re-layouts: 30.9 us -> 19.6 us
  other arithmetic: 10.8 us -> 21.1 us
    reduce_scatter x1 -> x0, waiting for transfers between devices: 161 us -> none  [body(): lax.psum_scatter(wg.reshape(nb * nd, d // nd, 3 * d), both, scatter_dimen...]
    ppermute x0 -> x30, waiting for transfers between devices: none -> 82.9 us  [the longest x18 51.2 us: flip(): lax.ppermute(a, axis, [(i, i ^ bit) for i in range(lax.axis_size(axis))])]
    unnamed x4 -> x1, waiting for transfers between devices: 79.8 us -> 0.02 us
    all_gather x1 -> x0, blocking collectives: 71.8 us -> none  [body(): sg = lax.all_gather(small, both, axis=0).reshape(nb, nd, -1)]
    all_gather x1, waiting for transfers between devices: 22.3 us -> 66.3 us  [body(): w = lax.all_gather(wl, both, axis=0).reshape(nb, d, 3 * d)]
    ppermute x0 -> x30, starting transfers between devices: none -> 31.5 us  [the longest x18 16.1 us: flip(): lax.ppermute(a, axis, [(i, i ^ bit) for i in range(lax.axis_size(axis))])]
    pallas_call x4, Pallas kernels: 69.9 us -> 41.9 us  [mem_forward(): pl.pallas_call(functools.partial(mem_forward_kernel, nmem, save), out_sha...]
    all_to_all x1 -> x0, blocking collectives: 14.2 us -> none  [body(): layer_out = lax.all_to_all(out.reshape(nb, part, d), 'mp', 0, 0, tiled=True)]
  transfers between devices with their start and end apart: 12 -> 41, of which waited for: 4 -> 20; matrix products, arithmetic and copies ran while one was open for 4% -> 6% of each run, Pallas kernels for 11% -> 21%
where the time goes in v2:
time: 481 us; the launch traced here: 472 us
  Pallas kernels  178 us (37%)
  waiting for transfers between devices  168 us (35%)
  starting transfers between devices  68 us (14%)
  other arithmetic  21.1 us (4%)
  local copies, waits for them, and re-layouts  19.6 us (4%)
  between operations  17.4 us (4%)
    all_gather x1, waiting for transfers between devices, body(): w = lax.all_gather(wl, both, axis=0).reshape(nb, d, 3 * d)  66.3 us
    pallas_call x1, Pallas kernels, token_call(): pl.pallas_call(functools.partial(token_kernel, nmem), out_shape=shapes, i...  59.8 us
    ppermute x18, waiting for transfers between devices, flip(): lax.ppermute(a, axis, [(i, i ^ bit) for i in range(lax.axis_size(axis))])  51.2 us
    pallas_call x4, Pallas kernels, mem_forward(): pl.pallas_call(functools.partial(mem_forward_kernel, nmem, save), out_sha...  41.9 us
    ppermute x12, waiting for transfers between devices, shift(): return lax.ppermute(a, 'dp', [(i, (i + by) % n) for i in range(n)])  31.7 us
    pallas_call x2, Pallas kernels, mem_backward(): pl.pallas_call(functools.partial(mem_backward_kernel, 0), out_shape=jax.S...  21.9 us
    ppermute x18, starting transfers between devices, flip(): lax.ppermute(a, axis, [(i, i ^ bit) for i in range(lax.axis_size(axis))])  16.1 us
    ppermute x12, starting transfers between devices, shift(): return lax.ppermute(a, 'dp', [(i, (i + by) % n) for i in range(n)])  15.4 us
  transfers between devices with their start and end apart: 41, of which 20 were waited for; matrix products, arithmetic and copies ran while one was open for 6% of the time, Pallas kernels for 21%

profile of v2, /device:TPU:0, one launch (start us, length us, event | category | flops | bytes accessed | tf_op | source)
XLA Modules:
  0.0 471.7 jit_solution(6233696351201095555)
XLA Ops:
  11.9 6.1 %concatenate.115 = bf16[768]{0:T(1024)(128)(2,1)S(1)} concatenate(bf16[24]{0:T(256)(128)(2,1)} %param.25, bf16[24]{0:T(256)(128)(2,1)} %param.28, bf16[96]{0:T(256)(128)(2,1)} %param.34, bf16[24]{0:T(256)(128)(2,1)} %param.30, bf16[24]{0:T(256)(128)(2,1)} %param.31, bf16[24]{0:T(256)(128)(2,1)} %param.32, bf16[24]{0:T(256)(128)(2,1)} %param.36, bf16[24]{0:T(256)(128)(2,1)} %param.37, ...), dimensions={0} | concatenate | bytes 3072 | tf_op jit(solution)/shard_map/concatenate | solution.py:977
  24.8 12.6 %collective-permute-done.1 = bf16[2,768]{1,0:T(2,128)(2,1)S(1)} collective-permute-done((bf16[2,768]{1,0:T(2,128)(2,1)S(1)}, bf16[2,768]{1,0:T(2,128)(2,1)S(1)}, u32[]{:S(2)}, u32[]{:S(2)}) %collective-permute-start.1) | collective-permute-done | bytes 3104 | tf_op jit(solution)/shard_map/ppermute | solution.py:882
  53.8 66.3 %all-gather.3.cloned.1.call-done = bf16[3072,2304]{1,0:T(8,128)(2,1)} async-done(((bf16[96,2304]{1,0:T(8,128)(2,1)}), bf16[3072,2304]{1,0:T(8,128)(2,1)}) %all-gather.3.cloned.1.call-update) | async-done | bytes 14155792 | tf_op jit(solution)/shard_map/all_gather | solution.py:975
  120.1 7.6 %qkv.1 = (bf16[4,512,256]{2,1,0:T(8,128)(2,1)}, bf16[4,512,256]{2,1,0:T(8,128)(2,1)}, bf16[4,512,256]{2,1,0:T(8,128)(2,1)}) custom-call(s32[1]{0:T(128)} %bitcast.me_ref, bf16[512,768]{1,0:T(8,128)(2,1)} %bitcast.235, bf16[4,768,2304]{2,1,0:T(8,128)(2,1)} %bitcast.217, f32[4,1,576]{2,1,0:T(1,128)} %pad_maximum_fusion.1.qkvb_ref), custom_call_target="tpu_custom_call" | custom-call | flops 1811939328 | bytes 4718592 | tf_op jit(solution)/shard_map/qkv/pallas_call | solution.py:137
  127.7 10.5 %mem_forward.3 = f32[32,768]{1,0:T(8,128)} custom-call(s32[1]{0:T(128)} %bitcast.me_ref, f32[32,768]{1,0:T(8,128)} %convert_select_fusion.m_ref, bf16[4,512,256]{2,1,0:T(8,128)(2,1)} %get-tuple-element.74.k_hbm, bf16[4,512,256]{2,1,0:T(8,128)(2,1)} %get-tuple-element.75.v_hbm, bf16[4,768,2304]{2,1,0:T(8,128)(2,1)} %bitcast.218, ...), custom_call_target="tpu_custom_call" | custom-call | flops 452984832 | bytes 14155776 | tf_op jit(solution)/shard_map/mem_forward/pallas_call | solution.py:256
  144.5 10.5 %mem_forward.4 = f32[32,768]{1,0:T(8,128)} custom-call(s32[1]{0:T(128)} %bitcast.me_ref, f32[32,768]{1,0:T(8,128)} %copy-done.6, bf16[4,512,256]{2,1,0:T(8,128)(2,1)} %get-tuple-element.74.k_hbm, bf16[4,512,256]{2,1,0:T(8,128)(2,1)} %get-tuple-element.75.v_hbm, bf16[4,768,2304]{2,1,0:T(8,128)(2,1)} %bitcast.219, f32[4,1,576]{2,1,0:T(1,128)} %pad_maximum_fusion.1.qkvb_ref, ...), custom_call_target="tpu_custom_call" | custom-call | flops 452984832 | bytes 14155776 | tf_op jit(solution)/shard_map/mem_forward/pallas_call | solution.py:256
  157.3 10.5 %mem_forward.5 = f32[32,768]{1,0:T(8,128)} custom-call(s32[1]{0:T(128)} %bitcast.me_ref, f32[32,768]{1,0:T(8,128)} %copy-done.8, bf16[4,512,256]{2,1,0:T(8,128)(2,1)} %get-tuple-element.74.k_hbm, bf16[4,512,256]{2,1,0:T(8,128)(2,1)} %get-tuple-element.75.v_hbm, bf16[4,768,2304]{2,1,0:T(8,128)(2,1)} %bitcast.220, f32[4,1,576]{2,1,0:T(1,128)} %pad_maximum_fusion.1.qkvb_ref, ...), custom_call_target="tpu_custom_call" | custom-call | flops 452984832 | bytes 14155776 | tf_op jit(solution)/shard_map/mem_forward/pallas_call | solution.py:256
  171.4 10.4 %mem_forward_save.1 = (f32[32,768]{1,0:T(8,128)}, bf16[4,32,256]{2,1,0:T(8,128)(2,1)}, bf16[4,32,256]{2,1,0:T(8,128)(2,1)}, bf16[4,32,256]{2,1,0:T(8,128)(2,1)},...) custom-call(s32[1]{0:T(128)} %bitcast.me_ref, ...), custom_call_target="tpu_custom_call" | custom-call | flops 452984832 | bytes 14155776 | tf_op jit(solution)/shard_map/mem_forward_save/pallas_call | solution.py:256
  182.7 59.8 %token_rows.1 = (bf16[512,768]{1,0:T(8,128)(2,1)}, bf16[512,768]{1,0:T(8,128)(2,1)}, bf16[4,512,256]{2,1,0:T(8,128)(2,1)}, bf16[4,512,768]{2,1,0:T(8,128)(2,1)},...) custom-call(s32[1]{0:T(128)} %bitcast.me_ref, ...), custom_call_target="tpu_custom_call" | custom-call | flops 18119393280 | bytes 35389440 | tf_op jit(solution)/shard_map/token_rows/pallas_call | solution.py:506
  242.4 9.8 %collective-permute-start.9 = (f32[32,768]{1,0:T(8,128)}, f32[32,768]{1,0:T(8,128)S(1)}, u32[]{:S(2)}, u32[]{:S(2)}) collective-permute-start(f32[32,768]{1,0:T(8,128)} %get-tuple-element.78.base_ref), channel_id=1, source_target_pairs={{3,2},{7,6},{11,10},{15,14},{19,18},{23,22},{27,26},{31,30}} | collective-permute-start | bytes 294920 | tf_op jit(solution)/shard_map/ppermute | solution.py:1014
  253.6 9.8 %all-to-all-start.2 = ((bf16[4,128,768]{2,1,0:T(8,128)(2,1)}), bf16[4,128,768]{2,1,0:T(8,128)(2,1)S(1)}, u32[]{:S(2)}, u32[]{:S(2)}) async-start(bf16[4,128,768]{2,1,0:T(8,128)(2,1)} %bitcast.243), calls=%async_computation.2 | async-start | bytes 1572864 | tf_op jit(solution)/shard_map/all_to_all | solution.py:1066
  264.0 10.9 %mem_backward.2 = f32[32,768]{1,0:T(8,128)} custom-call(s32[1]{0:T(128)} %bitcast.me_ref, f32[32,768]{1,0:T(8,128)} %copy-done.4, bf16[4,512,256]{2,1,0:T(8,128)(2,1)} %get-tuple-element.74.k_hbm, bf16[4,512,256]{2,1,0:T(8,128)(2,1)} %get-tuple-element.75.v_hbm, bf16[4,768,2304]{2,1,0:T(8,128)(2,1)} %bitcast.223, f32[8,768]{1,0:T(8,128)} %pad_convert_fusion.vec_ref, ...), custom_call_target="tpu_custom_call" | custom-call | flops 452984832 | bytes 14155776 | tf_op jit(solution)/shard_map/mem_backward/pallas_call | solution.py:607
  276.3 10.9 %mem_backward.3 = f32[32,768]{1,0:T(8,128)} custom-call(s32[1]{0:T(128)} %bitcast.me_ref, f32[32,768]{1,0:T(8,128)} %copy-done.9, bf16[4,512,256]{2,1,0:T(8,128)(2,1)} %get-tuple-element.74.k_hbm, bf16[4,512,256]{2,1,0:T(8,128)(2,1)} %get-tuple-element.75.v_hbm, bf16[4,768,2304]{2,1,0:T(8,128)(2,1)} %bitcast.224, f32[8,768]{1,0:T(8,128)} %pad_convert_fusion.vec_ref, ...), custom_call_target="tpu_custom_call" | custom-call | flops 452984832 | bytes 14155776 | tf_op jit(solution)/shard_map/mem_backward/pallas_call | solution.py:607
  288.5 6.9 %collective-permute-done.11 = f32[32,768]{1,0:T(8,128)S(1)} collective-permute-done((f32[32,768]{1,0:T(8,128)}, f32[32,768]{1,0:T(8,128)S(1)}, u32[]{:S(2)}, u32[]{:S(2)}) %collective-permute-start.11) | collective-permute-done | bytes 98336 | tf_op jit(solution)/shard_map/ppermute | solution.py:1014
  297.0 6.7 %last_feed.1 = (bf16[32,768]{1,0:T(8,128)(2,1)}, bf16[4,32,768]{2,1,0:T(8,128)(2,1)}, f32[32,768]{1,0:T(8,128)}, f32[8,768]{1,0:T(8,128)}, f32[4,1,768]{2,1,0:T(1,128)}) custom-call(s32[1]{0:T(128)} %bitcast.me_ref, f32[32,768]{1,0:T(8,128)} %add_add_fusion.g_ref, bf16[4,768,2304]{2,1,0:T(8,128)(2,1)} %bitcast.225, f32[8,768]{1,0:T(8,128)} %pad_convert_fusion.vec_ref, ...), custom_call_target="tpu_custom_call" | custom-call | flops 301989888 | bytes 9437184 | tf_op jit(solution)/shard_map/last_feed/pallas_call | solution.py:662
  303.6 13.2 %last_attention.1 = (f32[32,768]{1,0:T(8,128)}, bf16[4,544,576]{2,1,0:T(8,128)(2,1)}, bf16[512,768]{1,0:T(8,128)(2,1)}, f32[4,2,256]{2,1,0:T(2,128)}) custom-call(s32[1]{0:T(128)} %bitcast.me_ref, f32[32,768]{1,0:T(8,128)} %get-tuple-element.88.gr1m_ref, bf16[4,512,256]{2,1,0:T(8,128)(2,1)} %get-tuple-element.74.k_hbm, ...), custom_call_target="tpu_custom_call" | custom-call | flops 2415919104 | bytes 17694720 | tf_op jit(solution)/shard_map/last_attention/pallas_call | solution.py:739
  317.8 7.7 %feed_grad.2 = (bf16[2,768,768]{2,1,0:T(8,128)(2,1)}, bf16[2,768,768]{2,1,0:T(8,128)(2,1)}) custom-call(bf16[512,768]{1,0:T(8,128)(2,1)} %get-tuple-element.105.l_ref, bf16[32,768]{1,0:T(8,128)(2,1)} %get-tuple-element.106.lm_ref, bf16[4,512,768]{2,1,0:T(8,128)(2,1)} %get-tuple-element.107.r_ref, bf16[4,32,768]{2,1,0:T(8,128)(2,1)} %get-tuple-element.108.rm_ref), custom_call_target="tpu_custom_call" | custom-call | flops 2415919104 | bytes 9437184 | tf_op jit(solution)/shard_map/feed_grad/pallas_call | solution.py:783
  326.5 7.4 %feed_grad.3 = (bf16[2,768,768]{2,1,0:T(8,128)(2,1)}, bf16[2,768,768]{2,1,0:T(8,128)(2,1)}) custom-call(bf16[512,768]{1,0:T(8,128)(2,1)} %get-tuple-element.111.l_ref, bf16[32,768]{1,0:T(8,128)(2,1)} %get-tuple-element.112.lm_ref, bf16[4,512,768]{2,1,0:T(8,128)(2,1)} %get-tuple-element.113.r_ref, bf16[4,32,768]{2,1,0:T(8,128)(2,1)} %get-tuple-element.114.rm_ref), custom_call_target="tpu_custom_call" | custom-call | flops 2415919104 | bytes 9437184 | tf_op jit(solution)/shard_map/feed_grad/pallas_call | solution.py:783
  335.7 9.8 %attention_grad.1 = (bf16[2,8,104,768]{3,2,1,0:T(8,128)(2,1)}, bf16[2,8,104,768]{3,2,1,0:T(8,128)(2,1)}) custom-call(bf16[512,768]{1,0:T(8,128)(2,1)} %bitcast.237, f32[32,768]{1,0:T(8,128)} %add_add_fusion.1.m_ref, bf16[4,544,576]{2,1,0:T(8,128)(2,1)} %get-tuple-element.94.gqkv_ref, f32[512,768]{1,0:T(8,128)} %get-tuple-element.92.gr1_ref, ...), custom_call_target="tpu_custom_call" | custom-call | flops 2415919104 | bytes 9437184 | tf_op jit(solution)/shard_map/attention_grad/pallas_call | solution.py:835
  349.4 11.5 %all-to-all-done.3 = bf16[4,128,768]{2,1,0:T(8,128)(2,1)S(1)} async-done(((bf16[4,128,768]{2,1,0:T(8,128)(2,1)}), bf16[4,128,768]{2,1,0:T(8,128)(2,1)S(1)}, u32[]{:S(2)}, u32[]{:S(2)}) %all-to-all-start.3) | async-done | bytes 786464 | tf_op jit(solution)/shard_map/all_to_all | solution.py:1067
  383.1 10.1 %collective-permute-done.31 = bf16[4,2,96,384]{3,2,1,0:T(8,128)(2,1)S(1)} collective-permute-done((bf16[4,2,96,384]{3,2,1,0:T(8,128)(2,1)S(1)}, bf16[4,2,96,384]{3,2,1,0:T(8,128)(2,1)S(1)}, u32[]{:S(2)}, u32[]{:S(2)}) %collective-permute-start.31) | collective-permute-done | bytes 589856 | tf_op jit(solution)/shard_map/ppermute | solution.py:882
  395.4 11.5 %collective-permute-done.15 = bf16[4,2,104,384]{3,2,1,0:T(8,128)(2,1)S(1)} collective-permute-done((bf16[4,2,104,384]{3,2,1,0:T(8,128)(2,1)S(1)}, bf16[4,2,104,384]{3,2,1,0:T(8,128)(2,1)S(1)}, u32[]{:S(2)}, u32[]{:S(2)}) %collective-permute-start.15) | collective-permute-done | bytes 639008 | tf_op jit(solution)/shard_map/ppermute | solution.py:882
  429.5 7.3 %collective-permute-done.27 = bf16[2,96,384]{2,1,0:T(8,128)(2,1)S(1)} collective-permute-done((bf16[2,96,384]{2,1,0:T(8,128)(2,1)S(1)}, bf16[2,96,384]{2,1,0:T(8,128)(2,1)S(1)}, u32[]{:S(2)}, u32[]{:S(2)}) %collective-permute-start.27) | collective-permute-done | bytes 147488 | tf_op jit(solution)/shard_map/ppermute | solution.py:887
  452.5 6.1 %collective-permute-done.19 = bf16[2,104,384]{2,1,0:T(8,128)(2,1)S(1)} collective-permute-done((bf16[2,104,384]{2,1,0:T(8,128)(2,1)S(1)}, bf16[2,104,384]{2,1,0:T(8,128)(2,1)S(1)}, u32[]{:S(2)}, u32[]{:S(2)}) %collective-permute-start.19) | collective-permute-done | bytes 159776 | tf_op jit(solution)/shard_map/ppermute | solution.py:887
  (221 shorter events, 120.5 us)
Async XLA Ops:
  7.2 112.9 %all-gather.3.cloned.1.call-start = ((), (), s32[]{:S(2)}) async-start(), calls=%async_computation.4 | async-start | bytes 14598144 | tf_op jit(solution)/shard_map/all_gather | solution.py:975
  18.5 35.3 %all-to-all-start = ((bf16[4,128,768]{2,1,0:T(8,128)(2,1)}), bf16[4,128,768]{2,1,0:T(8,128)(2,1)S(1)}, u32[]{:S(2)}, u32[]{:S(2)}) async-start(bf16[4,128,768]{2,1,0:T(8,128)(2,1)} %bitcast.242), calls=%async_computation | async-start | bytes 1572864 | tf_op jit(solution)/shard_map/all_to_all | solution.py:993
  22.5 14.9 %collective-permute-start.1 = (bf16[2,768]{1,0:T(2,128)(2,1)S(1)}, bf16[2,768]{1,0:T(2,128)(2,1)S(1)}, u32[]{:S(2)}, u32[]{:S(2)}) collective-permute-start(bf16[2,768]{1,0:T(2,128)(2,1)S(1)} %broadcast_select_fusion), channel_id=1, source_target_pairs={{0,2},{1,3},{2,0},{3,1},{4,6},{5,7},{6,4},{7,5},{8,10},{9,11},{10,... | collective-permute-start | bytes 9224 | tf_op jit(solution)/shard_map/ppermute | solution.py:882
  140.4 41.4 %all-to-all-start.1 = ((bf16[4,128,768]{2,1,0:T(8,128)(2,1)}), bf16[4,128,768]{2,1,0:T(8,128)(2,1)S(1)}, u32[]{:S(2)}, u32[]{:S(2)}) async-start(bf16[4,128,768]{2,1,0:T(8,128)(2,1)} %bitcast.3), calls=%async_computation.1 | async-start | bytes 1572864 | tf_op jit(solution)/shard_map/all_to_all | solution.py:994
  242.4 20.9 %collective-permute-start.9 = (f32[32,768]{1,0:T(8,128)}, f32[32,768]{1,0:T(8,128)S(1)}, u32[]{:S(2)}, u32[]{:S(2)}) collective-permute-start(f32[32,768]{1,0:T(8,128)} %get-tuple-element.78.base_ref), channel_id=1, source_target_pairs={{3,2},{7,6},{11,10},{15,14},{19,18},{23,22},{27,26},{31,30}} | collective-permute-start | bytes 294920 | tf_op jit(solution)/shard_map/ppermute | solution.py:1014
  253.6 92.0 %all-to-all-start.2 = ((bf16[4,128,768]{2,1,0:T(8,128)(2,1)}), bf16[4,128,768]{2,1,0:T(8,128)(2,1)S(1)}, u32[]{:S(2)}, u32[]{:S(2)}) async-start(bf16[4,128,768]{2,1,0:T(8,128)(2,1)} %bitcast.243), calls=%async_computation.2 | async-start | bytes 1572864 | tf_op jit(solution)/shard_map/all_to_all | solution.py:1066
  325.5 35.5 %collective-permute-start.20 = (bf16[2,8,96,768]{3,2,1,0:T(8,128)(2,1)}, bf16[2,8,96,768]{3,2,1,0:T(8,128)(2,1)}, u32[]{:S(2)}, u32[]{:S(2)}) collective-permute-start(bf16[2,8,96,768]{3,2,1,0:T(8,128)(2,1)} %bitcast.261), channel_id=1, source_target_pairs={{0,1},{1,0},{2,3},{3,2},{4,5},{5,4},{6,7},{7,6},{8,9},{9,8},{10,11... | collective-permute-start | bytes 7077896 | tf_op jit(solution)/shard_map/ppermute | solution.py:882
  333.9 32.3 %collective-permute-start.28 = (bf16[2,8,96,768]{3,2,1,0:T(8,128)(2,1)}, bf16[2,8,96,768]{3,2,1,0:T(8,128)(2,1)}, u32[]{:S(2)}, u32[]{:S(2)}) collective-permute-start(bf16[2,8,96,768]{3,2,1,0:T(8,128)(2,1)} %bitcast.262), channel_id=1, source_target_pairs={{0,1},{1,0},{2,3},{3,2},{4,5},{5,4},{6,7},{7,6},{8,9},{9,8},{10,11... | collective-permute-start | bytes 7077896 | tf_op jit(solution)/shard_map/ppermute | solution.py:882
  345.4 25.9 %collective-permute-start.12 = (bf16[2,8,104,768]{3,2,1,0:T(8,128)(2,1)}, bf16[2,8,104,768]{3,2,1,0:T(8,128)(2,1)}, u32[]{:S(2)}, u32[]{:S(2)}) collective-permute-start(bf16[2,8,104,768]{3,2,1,0:T(8,128)(2,1)} %get-tuple-element.104), channel_id=1, source_target_pairs={{0,1},{1,0},{2,3},{3,2},{4,5},{5,4},{6,7},{7,6},{8,9},{9,8},{10,11... | collective-permute-start | bytes 7667720 | tf_op jit(solution)/shard_map/ppermute | solution.py:882
  345.6 15.4 %all-to-all-start.3 = ((bf16[4,128,768]{2,1,0:T(8,128)(2,1)}), bf16[4,128,768]{2,1,0:T(8,128)(2,1)S(1)}, u32[]{:S(2)}, u32[]{:S(2)}) async-start(bf16[4,128,768]{2,1,0:T(8,128)(2,1)} %bitcast.21), calls=%async_computation.3 | async-start | bytes 1572864 | tf_op jit(solution)/shard_map/all_to_all | solution.py:1067
  364.3 16.3 %collective-permute-start.23 = (bf16[4,2,96,384]{3,2,1,0:T(8,128)(2,1)S(1)}, bf16[4,2,96,384]{3,2,1,0:T(8,128)(2,1)S(1)}, u32[]{:S(2)}, u32[]{:S(2)}) collective-permute-start(bf16[4,2,96,384]{3,2,1,0:T(8,128)(2,1)S(1)} %slice_bitcast_fusion.3), channel_id=1, source_target_pairs={{0,2},{1,3},{2,0},{3,1},{4,6},{5,7},{6,4},{7,5},{8,10},{9,11},{10,... | collective-permute-start | bytes 1769480 | tf_op jit(solution)/shard_map/ppermute | solution.py:882
  364.7 17.5 %collective-permute-start.21 = (bf16[2,4,96,384]{3,2,1,0:T(8,128)(2,1)S(1)}, bf16[2,4,96,384]{3,2,1,0:T(8,128)(2,1)S(1)}, u32[]{:S(2)}, u32[]{:S(2)}) collective-permute-start(bf16[2,4,96,384]{3,2,1,0:T(8,128)(2,1)S(1)} %dynamic-slice_bitcast_fusion.2), channel_id=1, source_target_pairs={{0,4},{4,0},{8,12},{12,8},{16,20},{20,16},{24,28},{28,24},{1,5},{5... | collective-permute-start | bytes 1769480 | tf_op jit(solution)/shard_map/ppermute | solution.py:882
  368.9 24.3 %collective-permute-start.31 = (bf16[4,2,96,384]{3,2,1,0:T(8,128)(2,1)S(1)}, bf16[4,2,96,384]{3,2,1,0:T(8,128)(2,1)S(1)}, u32[]{:S(2)}, u32[]{:S(2)}) collective-permute-start(bf16[4,2,96,384]{3,2,1,0:T(8,128)(2,1)S(1)} %slice_bitcast_fusion.1), channel_id=1, source_target_pairs={{0,2},{1,3},{2,0},{3,1},{4,6},{5,7},{6,4},{7,5},{8,10},{9,11},{10,... | collective-permute-start | bytes 1769480 | tf_op jit(solution)/shard_map/ppermute | solution.py:882
  370.7 23.1 %collective-permute-start.29 = (bf16[2,4,96,384]{3,2,1,0:T(8,128)(2,1)S(1)}, bf16[2,4,96,384]{3,2,1,0:T(8,128)(2,1)S(1)}, u32[]{:S(2)}, u32[]{:S(2)}) collective-permute-start(bf16[2,4,96,384]{3,2,1,0:T(8,128)(2,1)S(1)} %dynamic-slice_bitcast_fusion.1), channel_id=1, source_target_pairs={{0,4},{4,0},{8,12},{12,8},{16,20},{20,16},{24,28},{28,24},{1,5},{5... | collective-permute-start | bytes 1769480 | tf_op jit(solution)/shard_map/ppermute | solution.py:882
  374.0 32.9 %collective-permute-start.15 = (bf16[4,2,104,384]{3,2,1,0:T(8,128)(2,1)S(1)}, bf16[4,2,104,384]{3,2,1,0:T(8,128)(2,1)S(1)}, u32[]{:S(2)}, u32[]{:S(2)}) collective-permute-start(bf16[4,2,104,384]{3,2,1,0:T(8,128)(2,1)S(1)} %get-tuple-element.214), channel_id=1, source_target_pairs={{0,2},{1,3},{2,0},{3,1},{4,6},{5,7},{6,4},{7,5},{8,10},{9,11},{10,... | collective-permute-start | bytes 1916936 | tf_op jit(solution)/shard_map/ppermute | solution.py:882
  380.6 26.9 %collective-permute-start.13 = (bf16[2,4,104,384]{3,2,1,0:T(8,128)(2,1)S(1)}, bf16[2,4,104,384]{3,2,1,0:T(8,128)(2,1)S(1)}, u32[]{:S(2)}, u32[]{:S(2)}) collective-permute-start(bf16[2,4,104,384]{3,2,1,0:T(8,128)(2,1)S(1)} %dynamic-slice_bitcast_fusion), channel_id=1, source_target_pairs={{0,4},{4,0},{8,12},{12,8},{16,20},{20,16},{24,28},{28,24},{1,5},{5... | collective-permute-start | bytes 1916936 | tf_op jit(solution)/shard_map/ppermute | solution.py:882
  382.2 31.5 %collective-permute-start.24 = (bf16[4,96,384]{2,1,0:T(8,128)(2,1)S(1)}, bf16[4,96,384]{2,1,0:T(8,128)(2,1)S(1)}, u32[]{:S(2)}, u32[]{:S(2)}) collective-permute-start(bf16[4,96,384]{2,1,0:T(8,128)(2,1)S(1)} %dynamic-slice_bitcast_fusion.5), channel_id=1, source_target_pairs={{0,4},{4,0},{8,12},{12,8},{16,20},{20,16},{24,28},{28,24},{1,5},{5... | collective-permute-start | bytes 884744 | tf_op jit(solution)/shard_map/ppermute | solution.py:882
  393.2 20.0 %collective-permute-start.22 = (bf16[4,96,384]{2,1,0:T(8,128)(2,1)S(1)}, bf16[4,96,384]{2,1,0:T(8,128)(2,1)S(1)}, u32[]{:S(2)}, u32[]{:S(2)}) collective-permute-start(bf16[4,96,384]{2,1,0:T(8,128)(2,1)S(1)} %slice_bitcast_fusion.9), channel_id=1, source_target_pairs={{0,2},{1,3},{2,0},{3,1},{4,6},{5,7},{6,4},{7,5},{8,10},{9,11},{10,... | collective-permute-start | bytes 884744 | tf_op jit(solution)/shard_map/ppermute | solution.py:882
  393.7 27.3 %collective-permute-start.32 = (bf16[4,96,384]{2,1,0:T(8,128)(2,1)S(1)}, bf16[4,96,384]{2,1,0:T(8,128)(2,1)S(1)}, u32[]{:S(2)}, u32[]{:S(2)}) collective-permute-start(bf16[4,96,384]{2,1,0:T(8,128)(2,1)S(1)} %dynamic-slice_bitcast_fusion.4), channel_id=1, source_target_pairs={{0,4},{4,0},{8,12},{12,8},{16,20},{20,16},{24,28},{28,24},{1,5},{5... | collective-permute-start | bytes 884744 | tf_op jit(solution)/shard_map/ppermute | solution.py:882
  406.9 12.6 %collective-permute-start.30 = (bf16[4,96,384]{2,1,0:T(8,128)(2,1)S(1)}, bf16[4,96,384]{2,1,0:T(8,128)(2,1)S(1)}, u32[]{:S(2)}, u32[]{:S(2)}) collective-permute-start(bf16[4,96,384]{2,1,0:T(8,128)(2,1)S(1)} %slice_bitcast_fusion.7), channel_id=1, source_target_pairs={{0,2},{1,3},{2,0},{3,1},{4,6},{5,7},{6,4},{7,5},{8,10},{9,11},{10,... | collective-permute-start | bytes 884744 | tf_op jit(solution)/shard_map/ppermute | solution.py:882
  407.4 35.6 %collective-permute-start.16 = (bf16[4,104,384]{2,1,0:T(8,128)(2,1)S(1)}, bf16[4,104,384]{2,1,0:T(8,128)(2,1)S(1)}, u32[]{:S(2)}, u32[]{:S(2)}) collective-permute-start(bf16[4,104,384]{2,1,0:T(8,128)(2,1)S(1)} %dynamic-slice_bitcast_fusion.3), channel_id=1, source_target_pairs={{0,4},{4,0},{8,12},{12,8},{16,20},{20,16},{24,28},{28,24},{1,5},{5... | collective-permute-start | bytes 958472 | tf_op jit(solution)/shard_map/ppermute | solution.py:882
  413.2 30.0 %collective-permute-start.14 = (bf16[4,104,384]{2,1,0:T(8,128)(2,1)S(1)}, bf16[4,104,384]{2,1,0:T(8,128)(2,1)S(1)}, u32[]{:S(2)}, u32[]{:S(2)}) collective-permute-start(bf16[4,104,384]{2,1,0:T(8,128)(2,1)S(1)} %slice_bitcast_fusion.5), channel_id=1, source_target_pairs={{0,2},{1,3},{2,0},{3,1},{4,6},{5,7},{6,4},{7,5},{8,10},{9,11},{10,... | collective-permute-start | bytes 958472 | tf_op jit(solution)/shard_map/ppermute | solution.py:882
  421.1 15.8 %collective-permute-start.27 = (bf16[2,96,384]{2,1,0:T(8,128)(2,1)S(1)}, bf16[2,96,384]{2,1,0:T(8,128)(2,1)S(1)}, u32[]{:S(2)}, u32[]{:S(2)}) collective-permute-start(bf16[2,96,384]{2,1,0:T(8,128)(2,1)S(1)} %get-tuple-element.224), channel_id=1, source_target_pairs={{0,16},{4,20},{8,24},{12,28},{16,0},{20,4},{24,8},{28,12},{1,17},{... | collective-permute-start | bytes 442376 | tf_op jit(solution)/shard_map/ppermute | solution.py:887
  421.9 15.0 %collective-permute-start.33 = (bf16[2,96,384]{2,1,0:T(8,128)(2,1)S(1)}, bf16[2,96,384]{2,1,0:T(8,128)(2,1)S(1)}, u32[]{:S(2)}, u32[]{:S(2)}) collective-permute-start(bf16[2,96,384]{2,1,0:T(8,128)(2,1)S(1)} %get-tuple-element.219), channel_id=1, source_target_pairs={{0,8},{4,12},{8,16},{12,20},{16,24},{20,28},{24,0},{28,4},{1,9},{5... | collective-permute-start | bytes 442376 | tf_op jit(solution)/shard_map/ppermute | solution.py:887
  (34 other events, 330.2 us)
Sparse Core Ops, SparseCore 0:
  11.6 108.4 all-gather.2
